TPU v7x, 256 devices: a whole 4x4x8 slice. The times are simulated.
256 devices in a mesh: leaf: 32 (over y, z), lvl: 8 (over x, core).
Axes of the slice: x: 4, y: 4, z: 8, core: 2. Of those that a mesh axis runs over, the one named last changes fastest.
Arguments:
- targets: float32 [64, 131072], P(None, ('leaf', 'lvl')), may hold values from -6 to 6
- tree_pos: int32 [131072], P(('leaf', 'lvl')), may hold values from 0 to 131071, as said below
- coords: float32 [8, 131072], P(None, ('leaf', 'lvl')), may hold values from -5 to 5
- ubasis: float32 [1024, 64, 128], P(('leaf', 'lvl')), may hold values from -0.5 to 0.5
- transfer_one: float32 [1024, 64, 64], P(('leaf', 'lvl')), may hold values from -0.375 to 0.375
- transfer_two: float32 [256, 64, 64], P(('leaf', 'lvl')), may hold values from -0.25 to 0.25
- anchors_one: float32 [256, 8, 64], P(('leaf', 'lvl')), may hold values from -5 to 5
- anchors_two: float32 [32, 8, 64], P('leaf'), may hold values from -5 to 5
- near_list: int32 [1024, 7], P(('leaf', 'lvl')), may hold values from 0 to 1023, as said below
- far_one: int32 [256, 4], P(('leaf', 'lvl')), may hold values from 0 to 255, as said below
- far_two: int32 [32, 4], P('leaf'), may hold values from 0 to 31, as said below
Outputs:
- coeffs: float32 [64, 131072], P(None, ('leaf', 'lvl'))
- residual: float32 [64, 131072], P(None, ('leaf', 'lvl'))
Inputs may be any that keep to these rules, and one draw needn't show every extreme that they name: `tree_pos`: A permutation; of the 512 entries of each aligned block of user points, exactly 2 lie in each aligned block of 512 tree positions. near_list[near_list[c, k], k] = c and near_list[c, k] != c; the partner lies in the same window of 8 consecutive leaf clusters as c, windows starting at multiples of 8 for even k and at 4 plus such multiples for odd k, counted cyclically over the 1024 clusters. far_one[far_one[d, k], k] = d, far_one[d, k] != d, and far_one[d, k] // 8 = d // 8. far_two[far_two[e, k], k] = e and far_two[e, k] != e.
All inputs are finite; a program needn't handle non-finite values.
Results may differ from a plain program's by a relative error of at most 0.0003.
Values sent between devices are 32-bit elements; how exact they have to be, the bound alone decides.
A program may use at most 64 MiB of HBM per device.

v0:
```python
import jax
import jax.numpy as jnp
from jax import lax
from jax.sharding import PartitionSpec as P

DIM = 8
ITERS = 2


PRECISE = lax.Precision.HIGHEST
RIDGE = 1.0
EPSILON = 1e-06


def with_halo(array, sides, width):
    for axis, dim in sides:
        count, length = (lax.axis_size(axis), array.shape[dim])
        up = [(i, (i + 1) % count) for i in range(count)]
        down = [(j, i) for i, j in up]
        last = lax.slice_in_dim(array, length - width, length, axis=dim)
        leading = lax.slice_in_dim(array, 0, width, axis=dim)
        before = lax.ppermute(last, axis, up)
        after = lax.ppermute(leading, axis, down)
        array = jnp.concatenate([before, array, after], axis=dim)
    return array


def kernel_block(left_pts, right_pts):
    left_sq = jnp.sum(left_pts * left_pts, axis=1)
    right_sq = jnp.sum(right_pts * right_pts, axis=1)
    cross = jnp.einsum("bdm,bdn->bmn", left_pts, right_pts, precision=PRECISE)
    distance = left_sq[:, :, None] + right_sq[:, None, :] - 2.0 * cross
    return jnp.exp(-distance / DIM)


def residual_norm(resid_vec):
    return lax.psum(jnp.sum(resid_vec * resid_vec, axis=1), ("leaf", "lvl"))


def on_device(
    targets,
    tree_pos,
    coords,
    ubasis,
    transfer_one,
    transfer_two,
    anchors_one,
    anchors_two,
    near_list,
    far_one,
    far_two,
):
    rhs_cols, pts_dev = targets.shape
    leaf_count, rank_size, point_count = ubasis.shape
    coord_count = coords.shape[0]
    near_lists = near_list.shape[1]
    leaf_devices = lax.axis_size("leaf")
    lvl_devices = lax.axis_size("lvl")
    all_devices = lax.axis_size(("leaf", "lvl"))
    my_index = lax.axis_index(("leaf", "lvl"))
    total_clusters = leaf_count * all_devices
    destination = tree_pos // pts_dev
    send_order = jnp.argsort(destination, stable=True)
    send_vals = jnp.take(targets, send_order, axis=1).reshape(
        rhs_cols, leaf_devices, lvl_devices, -1
    )
    send_pos = (
        jnp.take(tree_pos, send_order).astype(jnp.float32).reshape(1, leaf_devices, lvl_devices, -1)
    )
    got_vals, got_pos = (
        lax.all_to_all(
            lax.all_to_all(send_vals, "leaf", split_axis=1, concat_axis=1, tiled=True),
            "lvl",
            split_axis=2,
            concat_axis=2,
            tiled=True,
        ),
        lax.all_to_all(
            lax.all_to_all(send_pos, "leaf", split_axis=1, concat_axis=1, tiled=True),
            "lvl",
            split_axis=2,
            concat_axis=2,
            tiled=True,
        ),
    )
    tree_slots = got_pos.reshape(-1).astype(jnp.int32) - my_index * pts_dev
    tree_vals = (
        jnp.zeros((rhs_cols, pts_dev), jnp.float32)
        .at[:, tree_slots]
        .set(got_vals.reshape(rhs_cols, pts_dev))
    )
    ext_coords = with_halo(coords, ((("leaf", "lvl"), 1),), pts_dev)
    ext_points = jnp.transpose(
        ext_coords.reshape(coord_count, 3 * leaf_count, point_count), (1, 0, 2)
    )
    own_points = ext_points[leaf_count : 2 * leaf_count]
    rel_index = (near_list - my_index * leaf_count + leaf_count) % total_clusters
    blocks = [kernel_block(own_points, own_points)]
    for column in range(near_lists):
        blocks.append(kernel_block(jnp.take(ext_points, rel_index[:, column], axis=0), own_points))
    near_scale = (point_count * (near_lists + 1)) ** (-0.5)
    lower_count = far_one.shape[1]
    upper_count = far_two.shape[1]
    lower_idx = far_one[0] % lvl_devices
    upper_idx = far_two[0]
    lvl_anchors = lax.all_gather(anchors_one, "lvl", axis=0, tiled=True)
    top_anchors = lax.all_gather(anchors_two, "leaf", axis=0, tiled=True)
    lower_coup = kernel_block(
        jnp.take(lvl_anchors, lower_idx, axis=0),
        jnp.broadcast_to(anchors_one, (lower_count, coord_count, rank_size)),
    )
    upper_coup = kernel_block(
        jnp.take(top_anchors, upper_idx, axis=0),
        jnp.broadcast_to(anchors_two, (upper_count, coord_count, rank_size)),
    )
    lower_scale = lower_count ** (-0.5)
    upper_scale = upper_count ** (-0.5)
    own_upper = transfer_two[0]

    def apply_operator(vector):
        extended = with_halo(vector, ((("leaf", "lvl"), 1),), pts_dev)
        ext_blocks = extended.reshape(rhs_cols, 3 * leaf_count, point_count)
        own_blocks = ext_blocks[:, leaf_count : 2 * leaf_count]
        near_sum = jnp.einsum("rcq,cqp->rcp", own_blocks, blocks[0], precision=PRECISE)
        for column in range(near_lists):
            partner_vals = jnp.take(ext_blocks, rel_index[:, column], axis=1)
            near_sum = near_sum + jnp.einsum(
                "rcq,cqp->rcp", partner_vals, blocks[column + 1], precision=PRECISE
            )
        leaf_skel = jnp.einsum("rcq,ckq->rck", own_blocks, ubasis, precision=PRECISE)
        lower_skel = jnp.einsum("rck,ckj->rj", leaf_skel, transfer_one, precision=PRECISE)
        upper_part = jnp.dot(lower_skel, own_upper, precision=PRECISE)
        lower_all = lax.all_gather(lower_skel[None], "lvl", axis=0, tiled=True)
        far_lower = jnp.zeros((rhs_cols, rank_size), jnp.float32)
        for column in range(lower_count):
            far_lower = far_lower + jnp.dot(
                lower_all[lower_idx[column]], lower_coup[column], precision=PRECISE
            )
        upper_skel = lax.psum(upper_part, "lvl")
        upper_all = lax.all_gather(upper_skel[None], "leaf", axis=0, tiled=True)
        far_upper = jnp.zeros((rhs_cols, rank_size), jnp.float32)
        for column in range(upper_count):
            far_upper = far_upper + jnp.dot(
                upper_all[upper_idx[column]], upper_coup[column], precision=PRECISE
            )
        level_pot = far_lower * lower_scale + jnp.einsum(
            "rj,kj->rk", far_upper * upper_scale, own_upper, precision=PRECISE
        )
        leaf_pot = jnp.einsum("rj,ckj->rck", level_pot, transfer_one, precision=PRECISE)
        far_out = jnp.einsum("rck,ckq->rcq", leaf_pot, ubasis, precision=PRECISE)
        return (near_sum * near_scale + far_out).reshape(rhs_cols, pts_dev)

    right_side = apply_operator(tree_vals)
    solution = jnp.zeros((rhs_cols, pts_dev), jnp.float32)
    resid_vec = right_side
    direction = right_side
    norm_now = residual_norm(resid_vec)
    for turn_index in range(ITERS):
        image_vec = apply_operator(direction)
        a_image = apply_operator(image_vec) + RIDGE * direction
        curvature = lax.psum(jnp.sum(direction * a_image, axis=1), ("leaf", "lvl"))
        step_size = norm_now / (curvature + EPSILON)
        solution = solution + step_size[:, None] * direction
        resid_vec = resid_vec - step_size[:, None] * a_image
        if turn_index + 1 < ITERS:
            fresh_norm = residual_norm(resid_vec)
            direction = resid_vec + (fresh_norm / (norm_now + EPSILON))[:, None] * direction
            norm_now = fresh_norm
    back_sol = jnp.take(solution, tree_slots, axis=1).reshape(
        rhs_cols, leaf_devices, lvl_devices, -1
    )
    back_res = jnp.take(resid_vec, tree_slots, axis=1).reshape(
        rhs_cols, leaf_devices, lvl_devices, -1
    )
    ret_sol, ret_res = (
        lax.all_to_all(
            lax.all_to_all(back_sol, "leaf", split_axis=1, concat_axis=1, tiled=True),
            "lvl",
            split_axis=2,
            concat_axis=2,
            tiled=True,
        ),
        lax.all_to_all(
            lax.all_to_all(back_res, "leaf", split_axis=1, concat_axis=1, tiled=True),
            "lvl",
            split_axis=2,
            concat_axis=2,
            tiled=True,
        ),
    )
    coeffs = (
        jnp.zeros((rhs_cols, pts_dev), jnp.float32)
        .at[:, send_order]
        .set(ret_sol.reshape(rhs_cols, pts_dev))
    )
    residual = (
        jnp.zeros((rhs_cols, pts_dev), jnp.float32)
        .at[:, send_order]
        .set(ret_res.reshape(rhs_cols, pts_dev))
    )
    return (coeffs, residual)


def solution(mesh):
    return jax.shard_map(
        on_device,
        mesh=mesh,
        in_specs=(
            P(None, ("leaf", "lvl")),
            P(("leaf", "lvl")),
            P(None, ("leaf", "lvl")),
            P(("leaf", "lvl"), None, None),
            P(("leaf", "lvl"), None, None),
            P(("leaf", "lvl"), None, None),
            P(("leaf", "lvl"), None, None),
            P("leaf", None, None),
            P(("leaf", "lvl"), None),
            P(("leaf", "lvl"), None),
            P("leaf", None),
        ),
        out_specs=(P(None, ("leaf", "lvl")), P(None, ("leaf", "lvl"))),
        check_vma=False,
    )
```

profile of v0, /device:TPU:1, one launch (start us, length us, event | category | flops | bytes accessed | tf_op | source)
XLA Modules:
  0.0 974.5 jit_solution(13188944828162396288)
XLA Ops:
  0.6 2.7 collective-permute-start
  4.7 3.8 sort.17
  9.2 3.5 gather_fusion
  13.7 10.6 %all-to-all-start = ((f32[1,32,8,2]{2,3,0,1:T(2,128)}), f32[1,32,8,2]{2,3,0,1:T(2,128)S(1)}, u32[]{:S(2)}, u32[]{:S(2)}) async-start(f32[1,32,8,2]{2,3,0,1:T(2,128)} %copy.233), calls=%async_computation | async-start | bytes 65536 | tf_op jit(solution)/shard_map/all_to_all | solution.py:79
  24.9 33.7 %all_gather.39 = f32[32,8,64]{2,1,0:T(8,128)S(1)} all-gather(f32[1,8,64]{2,1,0:T(8,128)S(1)} %copy-done.45), channel_id=1, replica_groups=mesh['leaf'=32,'lvl'=8] {'leaf'}, dimensions={0}, use_global_device_ids=true | all-gather | bytes 67584 | tf_op jit(solution)/shard_map/all_gather | solution.py:107
  59.3 27.1 %all_gather.37 = f32[8,8,64]{2,1,0:T(8,128)S(1)} all-gather(f32[1,8,64]{2,1,0:T(8,128)S(1)} %copy-done.46), channel_id=1, replica_groups=mesh['leaf'=32,'lvl'=8] {'lvl'}, dimensions={0}, use_global_device_ids=true | all-gather | bytes 18432 | tf_op jit(solution)/shard_map/all_gather | solution.py:106
  95.3 3.4 all-to-all-start.1
  112.3 6.8 all-to-all-start.2
  131.1 6.7 all-to-all-start.3
  139.1 3.9 all-to-all-done.3
  144.2 1.8 scatter_custom_fusion
  147.8 2.6 collective-permute-done.2
  150.4 2.5 collective-permute-done.3
  153.2 1.3 gather_fusion.5
  154.5 1.3 gather_fusion.7
  155.9 1.3 gather_fusion.9
  157.2 1.3 gather_fusion.11
  158.5 1.3 gather_fusion.13
  159.8 1.3 gather_fusion.15
  161.2 1.3 gather_fusion.17
  164.7 17.9 %all-gather = f32[512,64]{1,0:T(8,128)S(1)} all-gather(f32[64,64]{1,0:T(8,128)S(1)} %convolution_bitcast_fusion.19), channel_id=2, replica_groups=mesh['leaf'=32,'lvl'=8] {'lvl'}, dimensions={0}, use_global_device_ids=true | all-gather | bytes 147456 | tf_op jit(solution)/shard_map/all_gather | solution.py:133
  182.8 20.4 %psum.63 = f32[1,64,64]{2,1,0:T(8,128)S(1)} all-reduce(f32[1,64,64]{2,1,0:T(8,128)S(1)} %convolution_bitcast_fusion.18), channel_id=1, replica_groups=mesh['leaf'=32,'lvl'=8] {'lvl'}, use_global_device_ids=true, to_apply=%region_12.16 | all-reduce | flops 4096 | bytes 32768 | tf_op jit(solution)/shard_map/psum | solution.py:139
  203.2 38.2 %all_gather.38 = f32[32,64,64]{2,1,0:T(8,128)S(1)} all-gather(f32[1,64,64]{2,1,0:T(8,128)S(1)} %psum.63), channel_id=1, replica_groups=mesh['leaf'=32,'lvl'=8] {'leaf'}, dimensions={0}, use_global_device_ids=true | all-gather | bytes 540672 | tf_op jit(solution)/shard_map/all_gather | solution.py:140
  251.6 14.6 %collective-permute-start.5 = (f32[64,512]{1,0:T(8,128)}, f32[64,512]{1,0:T(8,128)}, u32[]{:S(2)}, u32[]{:S(2)}) collective-permute-start(f32[64,512]{1,0:T(8,128)} %copy_bitcast_fusion.3), channel_id=1, source_target_pairs={{1,0},{2,1},{3,2},{4,3},{5,4},{6,5},{7,6},{8,7},{9,8},{10,9},{11,1... | collective-permute-start | bytes 393224 | tf_op jit(solution)/shard_map/ppermute | solution.py:23
  268.4 14.9 %all-gather.1 = f32[512,64]{1,0:T(8,128)S(1)} all-gather(f32[64,64]{1,0:T(8,128)S(1)} %convolution_bitcast_fusion.17), channel_id=3, replica_groups=mesh['leaf'=32,'lvl'=8] {'lvl'}, dimensions={0}, use_global_device_ids=true | all-gather | bytes 147456 | tf_op jit(solution)/shard_map/all_gather | solution.py:133
  283.2 20.4 %psum.65 = f32[1,64,64]{2,1,0:T(8,128)S(1)} all-reduce(f32[1,64,64]{2,1,0:T(8,128)S(1)} %convolution_bitcast_fusion.16), channel_id=1, replica_groups=mesh['leaf'=32,'lvl'=8] {'lvl'}, use_global_device_ids=true, to_apply=%region_17.21 | all-reduce | flops 4096 | bytes 32768 | tf_op jit(solution)/shard_map/psum | solution.py:139
  303.6 36.7 %all_gather.41 = f32[32,64,64]{2,1,0:T(8,128)S(1)} all-gather(f32[1,64,64]{2,1,0:T(8,128)S(1)} %psum.65), channel_id=1, replica_groups=mesh['leaf'=32,'lvl'=8] {'leaf'}, dimensions={0}, use_global_device_ids=true | all-gather | bytes 540672 | tf_op jit(solution)/shard_map/all_gather | solution.py:140
  345.2 1.2 gather_fusion.18
  347.6 1.2 gather_fusion.20
  348.8 1.2 gather_fusion.21
  353.2 1.4 convolution_add_fusion.27
  359.0 15.5 %collective-permute-start.7 = (f32[64,512]{1,0:T(8,128)S(1)}, f32[64,512]{1,0:T(8,128)}, u32[]{:S(2)}, u32[]{:S(2)}) collective-permute-start(f32[64,512]{1,0:T(8,128)S(1)} %copy_bitcast_fusion.2), channel_id=1, source_target_pairs={{1,0},{2,1},{3,2},{4,3},{5,4},{6,5},{7,6},{8,7},{9,8},{10,9},{11,1... | collective-permute-start | bytes 393224 | tf_op jit(solution)/shard_map/ppermute | solution.py:23
  376.3 13.2 %all-gather.2 = f32[512,64]{1,0:T(8,128)S(1)} all-gather(f32[64,64]{1,0:T(8,128)S(1)} %convolution_bitcast_fusion.15), channel_id=4, replica_groups=mesh['leaf'=32,'lvl'=8] {'lvl'}, dimensions={0}, use_global_device_ids=true | all-gather | bytes 147456 | tf_op jit(solution)/shard_map/all_gather | solution.py:133
  389.5 20.4 %psum.66 = f32[1,64,64]{2,1,0:T(8,128)S(1)} all-reduce(f32[1,64,64]{2,1,0:T(8,128)S(1)} %convolution_bitcast_fusion.14), channel_id=1, replica_groups=mesh['leaf'=32,'lvl'=8] {'lvl'}, use_global_device_ids=true, to_apply=%region_18.22 | all-reduce | flops 4096 | bytes 32768 | tf_op jit(solution)/shard_map/psum | solution.py:139
  409.9 37.2 %all_gather.43 = f32[32,64,64]{2,1,0:T(8,128)S(1)} all-gather(f32[1,64,64]{2,1,0:T(8,128)S(1)} %psum.66), channel_id=1, replica_groups=mesh['leaf'=32,'lvl'=8] {'leaf'}, dimensions={0}, use_global_device_ids=true | all-gather | bytes 540672 | tf_op jit(solution)/shard_map/all_gather | solution.py:140
  454.4 1.2 gather_fusion.27
  457.9 1.2 gather_fusion.31
  459.1 1.4 convolution_add_fusion.20
  464.6 88.5 %all-reduce = (f32[64]{0:T(128)S(1)}, f32[64]{0:T(128)S(1)}) all-reduce(f32[64]{0:T(128)S(1)} %get-tuple-element.22, f32[64]{0:T(128)S(1)} %get-tuple-element.21), channel_id=1, replica_groups=mesh['leaf'=32,'lvl'=8] {'leaf','lvl'}, use_global_device_ids=true, to_apply=%region_16.20 | all-reduce | flops 128 | bytes 1024 | tf_op jit(solution)/shard_map/psum | solution.py:37
  553.4 73.4 %psum.68 = f32[64]{0:T(128)S(1)} all-reduce(f32[64]{0:T(128)S(1)} %multiply_reduce_fusion), channel_id=1, replica_groups=mesh['leaf'=32,'lvl'=8] {'leaf','lvl'}, use_global_device_ids=true, to_apply=%region_22.26 | all-reduce | flops 64 | bytes 512 | tf_op jit(solution)/shard_map/psum | solution.py:37
  627.9 1.9 collective-permute-done.8
  629.9 2.5 collective-permute-done.9
  633.4 1.2 gather_fusion.32
  640.4 1.2 gather_fusion.37
  643.7 17.8 %all-gather.3 = f32[512,64]{1,0:T(8,128)S(1)} all-gather(f32[64,64]{1,0:T(8,128)S(1)} %convolution_bitcast_fusion.13), channel_id=5, replica_groups=mesh['leaf'=32,'lvl'=8] {'lvl'}, dimensions={0}, use_global_device_ids=true | all-gather | bytes 147456 | tf_op jit(solution)/shard_map/all_gather | solution.py:133
  661.5 20.4 %psum.69 = f32[1,64,64]{2,1,0:T(8,128)S(1)} all-reduce(f32[1,64,64]{2,1,0:T(8,128)S(1)} %convolution_bitcast_fusion.12), channel_id=1, replica_groups=mesh['leaf'=32,'lvl'=8] {'lvl'}, use_global_device_ids=true, to_apply=%region_23.27 | all-reduce | flops 4096 | bytes 32768 | tf_op jit(solution)/shard_map/psum | solution.py:139
  681.8 38.3 %all_gather.45 = f32[32,64,64]{2,1,0:T(8,128)S(1)} all-gather(f32[1,64,64]{2,1,0:T(8,128)S(1)} %psum.69), channel_id=1, replica_groups=mesh['leaf'=32,'lvl'=8] {'leaf'}, dimensions={0}, use_global_device_ids=true | all-gather | bytes 540672 | tf_op jit(solution)/shard_map/all_gather | solution.py:140
  729.0 14.7 %collective-permute-start.11 = (f32[64,512]{1,0:T(8,128)S(1)}, f32[64,512]{1,0:T(8,128)}, u32[]{:S(2)}, u32[]{:S(2)}) collective-permute-start(f32[64,512]{1,0:T(8,128)S(1)} %copy_bitcast_fusion.1), channel_id=1, source_target_pairs={{1,0},{2,1},{3,2},{4,3},{5,4},{6,5},{7,6},{8,7},{9,8},{10,9},{11,1... | collective-permute-start | bytes 393224 | tf_op jit(solution)/shard_map/ppermute | solution.py:23
  745.5 14.7 %all-gather.4 = f32[512,64]{1,0:T(8,128)S(1)} all-gather(f32[64,64]{1,0:T(8,128)S(1)} %convolution_bitcast_fusion.11), channel_id=6, replica_groups=mesh['leaf'=32,'lvl'=8] {'lvl'}, dimensions={0}, use_global_device_ids=true | all-gather | bytes 147456 | tf_op jit(solution)/shard_map/all_gather | solution.py:133
  760.2 20.4 %psum.70 = f32[1,64,64]{2,1,0:T(8,128)S(1)} all-reduce(f32[1,64,64]{2,1,0:T(8,128)S(1)} %convolution_bitcast_fusion.10), channel_id=1, replica_groups=mesh['leaf'=32,'lvl'=8] {'lvl'}, use_global_device_ids=true, to_apply=%region_24.28 | all-reduce | flops 4096 | bytes 32768 | tf_op jit(solution)/shard_map/psum | solution.py:139
  780.6 37.0 %all_gather.47 = f32[32,64,64]{2,1,0:T(8,128)S(1)} all-gather(f32[1,64,64]{2,1,0:T(8,128)S(1)} %psum.70), channel_id=1, replica_groups=mesh['leaf'=32,'lvl'=8] {'leaf'}, dimensions={0}, use_global_device_ids=true | all-gather | bytes 540672 | tf_op jit(solution)/shard_map/all_gather | solution.py:140
  824.9 1.2 gather_fusion.45
  826.1 1.3 convolution_add_fusion.6
  830.6 87.9 %psum.71 = f32[64]{0:T(128)S(1)} all-reduce(f32[64]{0:T(128)S(1)} %get-tuple-element.50), channel_id=1, replica_groups=mesh['leaf'=32,'lvl'=8] {'leaf','lvl'}, use_global_device_ids=true, to_apply=%region_26.30 | all-reduce | flops 64 | bytes 512 | tf_op jit(solution)/shard_map/psum | solution.py:161
  922.1 4.6 all-to-all-start.6
  927.6 8.2 all-to-all-done.6
  935.8 3.9 all-to-all-start.4
  941.8 7.0 all-to-all-done.4
  948.9 6.6 all-to-all-start.7
  957.6 3.2 all-to-all-done.7
  960.7 4.1 all-to-all-start.5
  966.1 1.9 scatter_custom_fusion.2
  968.8 1.4 all-to-all-done.5
  971.4 1.9 scatter_custom_fusion.1
  (409 shorter events, 114.5 us)
Async XLA Ops:
  0.6 162.9 %copy-start = (f32[4,64,128]{2,1,0:T(8,128)S(1)}, f32[4,64,128]{2,1,0:T(8,128)}, u32[]{:S(2)}) copy-start(f32[4,64,128]{2,1,0:T(8,128)} %param.20) | copy-start | bytes 393220
  0.6 119.5 %collective-permute-start = (f32[8,512]{1,0:T(8,128)}, f32[8,512]{1,0:T(8,128)S(1)}, u32[]{:S(2)}, u32[]{:S(2)}) collective-permute-start(f32[8,512]{1,0:T(8,128)} %param.19), channel_id=1, source_target_pairs={{0,1},{1,2},{2,3},{3,4},{4,5},{5,6},{6,7},{7,8},{8,9},{9,10},{10,1... | collective-permute-start | bytes 49160 | tf_op jit(solution)/shard_map/ppermute | solution.py:22
  3.3 116.9 %collective-permute-start.1 = (f32[8,512]{1,0:T(8,128)}, f32[8,512]{1,0:T(8,128)S(1)}, u32[]{:S(2)}, u32[]{:S(2)}) collective-permute-start(f32[8,512]{1,0:T(8,128)} %param.19), channel_id=1, source_target_pairs={{1,0},{2,1},{3,2},{4,3},{5,4},{6,5},{7,6},{8,7},{9,8},{10,9},{11,1... | collective-permute-start | bytes 49160 | tf_op jit(solution)/shard_map/ppermute | solution.py:23
  13.7 10.6 %copy-start.65 = (s32[4,7]{1,0:T(4,128)S(1)}, s32[4,7]{1,0:T(4,128)}, u32[]{:S(2)}) copy-start(s32[4,7]{1,0:T(4,128)} %param.25) | copy-start | bytes 340
  13.7 11.1 %copy-start.64 = (s32[1,4]{1,0:T(1,128)S(1)}, s32[1,4]{1,0:T(1,128)}, u32[]{:S(2)}) copy-start(s32[1,4]{1,0:T(1,128)} %param.27) | copy-start | bytes 52
  13.7 11.1 %copy-start.45 = (f32[1,8,64]{2,1,0:T(8,128)S(1)}, f32[1,8,64]{2,1,0:T(8,128)}, u32[]{:S(2)}) copy-start(f32[1,8,64]{2,1,0:T(8,128)} %param.24) | copy-start | bytes 6148
  13.7 80.9 %all-to-all-start = ((f32[1,32,8,2]{2,3,0,1:T(2,128)}), f32[1,32,8,2]{2,3,0,1:T(2,128)S(1)}, u32[]{:S(2)}, u32[]{:S(2)}) async-start(f32[1,32,8,2]{2,3,0,1:T(2,128)} %copy.233), calls=%async_computation | async-start | bytes 65536 | tf_op jit(solution)/shard_map/all_to_all | solution.py:79
  24.4 62.1 %copy-start.36 = (f32[64,512]{1,0:T(8,128)S(1)}, f32[64,512]{1,0:T(8,128)}, u32[]{:S(2)}) copy-start(f32[64,512]{1,0:T(8,128)} %param.17) | copy-start | bytes 393220
  24.7 96.8 %copy-start.43 = (pred[4]{0:T(512)(128)(4,1)}, pred[4]{0:T(512)(128)(4,1)S(1)}, u32[]{:S(2)}) copy-start(pred[4]{0:T(512)(128)(4,1)S(1)} %compare_and_fusion.7) | copy-start | bytes 16
  24.8 97.5 %copy-start.39 = (pred[4]{0:T(512)(128)(4,1)}, pred[4]{0:T(512)(128)(4,1)S(1)}, u32[]{:S(2)}) copy-start(pred[4]{0:T(512)(128)(4,1)S(1)} %get-tuple-element.63) | copy-start | bytes 16
  24.8 100.2 %copy-start.37 = (pred[4]{0:T(512)(128)(4,1)}, pred[4]{0:T(512)(128)(4,1)S(1)}, u32[]{:S(2)}) copy-start(pred[4]{0:T(512)(128)(4,1)S(1)} %get-tuple-element.61) | copy-start | bytes 16
  24.9 34.4 %copy-start.66 = (s32[1,4]{1,0:T(1,128)S(1)}, s32[1,4]{1,0:T(1,128)}, u32[]{:S(2)}) copy-start(s32[1,4]{1,0:T(1,128)} %param.26) | copy-start | bytes 52
  87.6 32.6 %copy-start.48 = (s32[1024]{0:T(1024)}, s32[1024]{0:T(1024)S(1)}, u32[]{:S(2)}) copy-start(s32[1024]{0:T(1024)S(1)} %pad_clamp_fusion.9) | copy-start | bytes 12292
  87.6 33.2 %copy-start.50 = (s32[1024]{0:T(1024)}, s32[1024]{0:T(1024)S(1)}, u32[]{:S(2)}) copy-start(s32[1024]{0:T(1024)S(1)} %pad_clamp_fusion.8) | copy-start | bytes 12292
  87.7 35.3 %copy-start.52 = (s32[1024]{0:T(1024)}, s32[1024]{0:T(1024)S(1)}, u32[]{:S(2)}) copy-start(s32[1024]{0:T(1024)S(1)} %pad_clamp_fusion.7) | copy-start | bytes 12292
  87.7 36.7 %copy-start.54 = (s32[1024]{0:T(1024)}, s32[1024]{0:T(1024)S(1)}, u32[]{:S(2)}) copy-start(s32[1024]{0:T(1024)S(1)} %pad_clamp_fusion.6) | copy-start | bytes 12292
  87.7 38.0 %copy-start.56 = (s32[1024]{0:T(1024)}, s32[1024]{0:T(1024)S(1)}, u32[]{:S(2)}) copy-start(s32[1024]{0:T(1024)S(1)} %pad_clamp_fusion.5) | copy-start | bytes 12292
  87.7 39.4 %copy-start.58 = (s32[1024]{0:T(1024)}, s32[1024]{0:T(1024)S(1)}, u32[]{:S(2)}) copy-start(s32[1024]{0:T(1024)S(1)} %pad_clamp_fusion.4) | copy-start | bytes 12292
  92.1 46.3 %copy-start.60 = (s32[1024]{0:T(1024)}, s32[1024]{0:T(1024)S(1)}, u32[]{:S(2)}) copy-start(s32[1024]{0:T(1024)S(1)} %pad_clamp_fusion.3) | copy-start | bytes 12292
  95.3 17.1 %all-to-all-start.1 = ((f32[1,32,8,2]{1,3,0,2:T(2,128)}), f32[1,32,8,2]{1,3,0,2:T(2,128)S(1)}, u32[]{:S(2)}, u32[]{:S(2)}) async-start(f32[1,32,8,2]{1,3,0,2:T(2,128)} %copy.234), calls=%async_computation.1 | async-start | bytes 16384 | tf_op jit(solution)/shard_map/all_to_all | solution.py:78
  112.3 16.0 %all-to-all-start.2 = ((f32[32,1,1024]{2,1,0:T(1,128)}), f32[32,1,1024]{2,1,0:T(1,128)S(1)}, u32[]{:S(2)}, u32[]{:S(2)}) async-start(f32[32,1,1024]{2,1,0:T(1,128)} %reshape.858), calls=%async_computation.2 | async-start | bytes 262144 | tf_op jit(solution)/shard_map/all_to_all | solution.py:72
  131.1 11.9 %all-to-all-start.3 = ((f32[8,1,4096]{2,1,0:T(1,128)}), f32[8,1,4096]{2,1,0:T(1,128)S(1)}, u32[]{:S(2)}, u32[]{:S(2)}) async-start(f32[8,1,4096]{2,1,0:T(1,128)} %reshape.860), calls=%async_computation.3 | async-start | bytes 262144 | tf_op jit(solution)/shard_map/all_to_all | solution.py:71
  146.0 4.4 collective-permute-start.2
  147.1 5.8 collective-permute-start.3
  163.5 0.9 copy-start.2
  164.7 18.0 %copy-start.5 = (f32[1,64,64]{2,1,0:T(8,128)S(1)}, f32[1,64,64]{2,1,0:T(8,128)}, u32[]{:S(2)}) copy-start(f32[1,64,64]{2,1,0:T(8,128)} %param.22) | copy-start | bytes 49156
  203.2 38.2 %copy-start.4 = (f32[4,64,64]{2,1,0:T(8,128)S(1)}, f32[4,64,64]{2,1,0:T(8,128)}, u32[]{:S(2)}) copy-start(f32[4,64,64]{2,1,0:T(8,128)} %fusion.50) | copy-start | bytes 196612
  241.8 0.9 copy-start.3
  244.1 0.9 copy-start.23
  244.1 1.0 copy-start.34
  244.1 1.0 copy-start.44
  245.1 0.9 copy-start.40
  251.6 91.1 %collective-permute-start.5 = (f32[64,512]{1,0:T(8,128)}, f32[64,512]{1,0:T(8,128)}, u32[]{:S(2)}, u32[]{:S(2)}) collective-permute-start(f32[64,512]{1,0:T(8,128)} %copy_bitcast_fusion.3), channel_id=1, source_target_pairs={{1,0},{2,1},{3,2},{4,3},{5,4},{6,5},{7,6},{8,7},{9,8},{10,9},{11,1... | collective-permute-start | bytes 393224 | tf_op jit(solution)/shard_map/ppermute | solution.py:23
  266.1 77.5 %collective-permute-start.4 = (f32[64,512]{1,0:T(8,128)}, f32[64,512]{1,0:T(8,128)}, u32[]{:S(2)}, u32[]{:S(2)}) collective-permute-start(f32[64,512]{1,0:T(8,128)} %copy_bitcast_fusion.3), channel_id=1, source_target_pairs={{0,1},{1,2},{2,3},{3,4},{4,5},{5,6},{6,7},{7,8},{8,9},{9,10},{10,1... | collective-permute-start | bytes 393224 | tf_op jit(solution)/shard_map/ppermute | solution.py:22
  345.2 1.2 copy-start.51
  346.4 1.2 copy-start.53
  347.6 1.2 copy-start.55
  348.8 1.2 copy-start.57
  350.1 1.2 copy-start.59
  353.2 1.4 copy-start.30
  354.6 0.9 copy-start.28
  357.7 0.9 copy-start.24
  359.0 91.1 %collective-permute-start.7 = (f32[64,512]{1,0:T(8,128)S(1)}, f32[64,512]{1,0:T(8,128)}, u32[]{:S(2)}, u32[]{:S(2)}) collective-permute-start(f32[64,512]{1,0:T(8,128)S(1)} %copy_bitcast_fusion.2), channel_id=1, source_target_pairs={{1,0},{2,1},{3,2},{4,3},{5,4},{6,5},{7,6},{8,7},{9,8},{10,9},{11,1... | collective-permute-start | bytes 393224 | tf_op jit(solution)/shard_map/ppermute | solution.py:23
  374.5 76.5 %collective-permute-start.6 = (f32[64,512]{1,0:T(8,128)S(1)}, f32[64,512]{1,0:T(8,128)}, u32[]{:S(2)}, u32[]{:S(2)}) collective-permute-start(f32[64,512]{1,0:T(8,128)S(1)} %copy_bitcast_fusion.2), channel_id=1, source_target_pairs={{0,1},{1,2},{2,3},{3,4},{4,5},{5,6},{6,7},{7,8},{8,9},{9,10},{10,1... | collective-permute-start | bytes 393224 | tf_op jit(solution)/shard_map/ppermute | solution.py:22
  459.1 1.4 copy-start.31
  460.5 0.9 copy-start.29
  463.2 0.9 copy-start.8
  463.2 1.0 copy-start.9
  464.6 88.7 %copy-start.6 = (f32[64,4,128]{2,0,1:T(8,128)}, f32[64,4,128]{2,0,1:T(8,128)S(1)}, u32[]{:S(2)}) copy-start(f32[64,4,128]{2,0,1:T(8,128)S(1)} %get-tuple-element.32) | copy-start | bytes 393220
  626.7 1.2 copy-start.42
  626.8 1.1 copy-start.63
  626.8 3.0 collective-permute-start.8
  627.9 4.5 collective-permute-start.9
  722.2 0.9 copy-start.22
  722.2 1.0 copy-start.33
  729.0 91.5 %collective-permute-start.11 = (f32[64,512]{1,0:T(8,128)S(1)}, f32[64,512]{1,0:T(8,128)}, u32[]{:S(2)}, u32[]{:S(2)}) collective-permute-start(f32[64,512]{1,0:T(8,128)S(1)} %copy_bitcast_fusion.1), channel_id=1, source_target_pairs={{1,0},{2,1},{3,2},{4,3},{5,4},{6,5},{7,6},{8,7},{9,8},{10,9},{11,1... | collective-permute-start | bytes 393224 | tf_op jit(solution)/shard_map/ppermute | solution.py:23
  743.7 77.8 %collective-permute-start.10 = (f32[64,512]{1,0:T(8,128)S(1)}, f32[64,512]{1,0:T(8,128)S(1)}, u32[]{:S(2)}, u32[]{:S(2)}) collective-permute-start(f32[64,512]{1,0:T(8,128)S(1)} %copy_bitcast_fusion.1), channel_id=1, source_target_pairs={{0,1},{1,2},{2,3},{3,4},{4,5},{5,6},{6,7},{7,8},{8,9},{9,10},{10,1... | collective-permute-start | bytes 393224 | tf_op jit(solution)/shard_map/ppermute | solution.py:22
  829.0 0.9 copy-start.7
  829.1 1.0 copy-start.32
  829.1 1.0 copy-start.35
  922.1 13.8 %all-to-all-start.6 = ((f32[32,1,1024]{2,1,0:T(1,128)}), f32[32,1,1024]{2,1,0:T(1,128)S(1)}, u32[]{:S(2)}, u32[]{:S(2)}) async-start(f32[32,1,1024]{2,1,0:T(1,128)} %reshape.866), calls=%async_computation.6 | async-start | bytes 262144 | tf_op jit(solution)/shard_map/all_to_all | solution.py:184
  935.8 13.0 %all-to-all-start.4 = ((f32[32,1,1024]{2,1,0:T(1,128)}), f32[32,1,1024]{2,1,0:T(1,128)S(1)}, u32[]{:S(2)}, u32[]{:S(2)}) async-start(f32[32,1,1024]{2,1,0:T(1,128)} %reshape.862), calls=%async_computation.4 | async-start | bytes 262144 | tf_op jit(solution)/shard_map/all_to_all | solution.py:177
  948.9 11.9 %all-to-all-start.7 = ((f32[8,1,4096]{2,1,0:T(1,128)}), f32[8,1,4096]{2,1,0:T(1,128)S(1)}, u32[]{:S(2)}, u32[]{:S(2)}) async-start(f32[8,1,4096]{2,1,0:T(1,128)} %reshape.868), calls=%async_computation.7 | async-start | bytes 262144 | tf_op jit(solution)/shard_map/all_to_all | solution.py:183
  960.7 9.4 all-to-all-start.5
  (23 other events, 19.2 us)
where the time goes:
time: 985 us; the launch traced here: 974 us
  blocking collectives  679 us (69%)
  starting transfers between devices  97.4 us (10%)
  local copies, waits for them, and re-layouts  87.3 us (9%)
  matrix products  46.3 us (5%)
  waiting for transfers between devices  33.2 us (3%)
  between operations  18.3 us (2%)
  other arithmetic  13.4 us (1%)
    all_gather x5, blocking collectives, apply_operator(): upper_all = lax.all_gather(upper_skel[None], 'leaf', axis=0, tiled=True)  187 us
    psum x2, blocking collectives, residual_norm(): return lax.psum(jnp.sum(resid_vec * resid_vec, axis=1), ('leaf', 'lvl'))  162 us
    psum x5, blocking collectives, apply_operator(): upper_skel = lax.psum(upper_part, 'lvl')  102 us
    psum x1, blocking collectives, on_device(): curvature = lax.psum(jnp.sum(direction * a_image, axis=1), ('leaf', 'lvl'))  87.9 us
    all_gather x5, blocking collectives, apply_operator(): lower_all = lax.all_gather(lower_skel[None], 'lvl', axis=0, tiled=True)  78.5 us
    ppermute x6, starting transfers between devices, with_halo(): after = lax.ppermute(leading, axis, down)  45.5 us
    gather x35, local copies, waits for them, and re-layouts, apply_operator(): partner_vals = jnp.take(ext_blocks, rel_index[:, column], axis=1)  37.2 us
    all_gather x1, blocking collectives, on_device(): top_anchors = lax.all_gather(anchors_two, 'leaf', axis=0, tiled=True)  33.7 us
  transfers between devices with their start and end apart: 20, of which 9 were waited for; matrix products, arithmetic and copies ran while one was open for 5% of the time, Pallas kernels for 0%

commit v1 on v0

v1 whole, which is shorter than its diff:
```python
import jax
import jax.numpy as jnp
from jax import lax
from jax.experimental import pallas as pl
from jax.experimental.pallas import tpu as pltpu
from jax.sharding import PartitionSpec as P

F32 = jnp.float32
BF16 = jnp.bfloat16
MESH = pl.DeviceIdType.MESH
PRECISE = lax.Precision.HIGHEST
DIM = 8
RIDGE = 1.0
EPSILON = 1e-6
APPLIES = 5
LANES = 128


def dot(a, b, ca=1, cb=0):
    return lax.dot_general(a, b, (((ca,), (cb,)), ((), ())), preferred_element_type=F32)


def dot_precise(a, b):
    return lax.dot_general(
        a, b, (((1,), (0,)), ((), ())), precision=PRECISE, preferred_element_type=F32
    )


def split2(x):
    hi = x.astype(BF16)
    return hi, (x - hi.astype(F32)).astype(BF16)


def split3(x):
    hi = x.astype(BF16)
    rest = x - hi.astype(F32)
    mid = rest.astype(BF16)
    return hi, mid, (rest - mid.astype(F32)).astype(BF16)


def dot_split(a, b_hi, b_lo):
    rows = a.shape[0]
    a_hi, a_lo = split2(a)
    both = dot(jnp.concatenate([a_hi, a_lo], axis=0), b_hi)
    return both[:rows] + both[rows:] + dot(a_hi, b_lo)


def iota(shape, dim):
    return lax.broadcasted_iota(jnp.int32, shape, dim)


def augmented(x):
    n = x.shape[1]
    x1, x2, x3 = (p.astype(F32) for p in split3(x))
    sq = jnp.sum(x * x, axis=0, keepdims=True) * (-1.0 / DIM)
    n1, n2, n3 = (p.astype(F32) for p in split3(sq))
    row = iota((8, n), 0)
    lead = jnp.where(row == 0, n1, jnp.where(row == 1, n2, n3))
    tail = jnp.where(row == 3, n1, jnp.where(row == 4, n2, n3))
    zero = jnp.zeros((8, n), F32)
    src_norm = jnp.where(row < 3, lead, jnp.where(row < 6, 1.0, 0.0))
    dst_norm = jnp.where(row < 3, 1.0, jnp.where(row < 6, tail, 0.0))
    q = 2.0 / DIM
    src = jnp.concatenate([x1, x1, x2, x1, x3, x2, src_norm, zero], axis=0)
    dst = jnp.concatenate([x1 * q, x2 * q, x1 * q, x3 * q, x1 * q, x2 * q, dst_norm, zero], axis=0)
    return src, dst


def pack(onehot, x):
    total = None
    for part in split3(x):
        zero = jnp.zeros_like(part)
        wide = jnp.concatenate(
            [jnp.concatenate([part, zero], axis=1), jnp.concatenate([zero, part], axis=1)], axis=0
        )
        term = dot(onehot, wide, 1, 1)
        total = term if total is None else total + term
    return total


def unpack(onehot, g):
    half = g.shape[1] // 2
    cols = onehot.shape[1] // 2
    gt = jnp.transpose(g)
    total = None
    for part in split3(gt):
        term = dot(part, onehot)
        total = term if total is None else total + term
    return total[:half, :cols] + total[half:, cols:]


def kernel(
    sizes,
    targets, tree_pos, coords, ubasis, transfer_one, transfer_two, anchors_one, anchors_two,
    near_list, far_one, far_two,
    coeffs, residual,
    oh_user, oh_tree, s_a, r_a, s_b, r_b, s_c, r_c, s_d, r_d,
    r_coords, s_anch, r_anch, s_top, r_top,
    src_pts, w_hi, w_lo, k1_hi, k1_lo, k2_hi, k2_lo, c_hi, c_lo, ct_hi, ct_lo,
    vbuf, pbuf, acc, r_halo, s1, r1, s2, r2, s3, r3, step_ref, norm_ref,
    set_send, set_recv, send_sem, halo_sem, stage_sem,
):
    n_leaf, n_lvl = sizes
    leaf, lvl = lax.axis_index("leaf"), lax.axis_index("lvl")
    rows, pts = targets.shape
    clusters = ubasis.shape[0]
    points = ubasis.shape[2]
    total = n_leaf * n_lvl * clusters
    near_lists = near_list.shape[1]

    def lvl_peer(k):
        return lax.rem(lvl + k, n_lvl)

    def leaf_peer(k):
        return lax.rem(leaf + k, n_leaf)

    ring = leaf * n_lvl + lvl
    n_all = n_leaf * n_lvl
    after = lax.rem(ring + 1, n_all)
    before = lax.rem(ring + n_all - 1, n_all)
    after_id = (after // n_lvl, lax.rem(after, n_lvl))
    before_id = (before // n_lvl, lax.rem(before, n_lvl))

    def copy(src, dst, send, recv, device):
        pltpu.make_async_remote_copy(
            src_ref=src, dst_ref=dst, send_sem=send, recv_sem=recv,
            device_id=device, device_id_type=MESH,
        ).start()

    def wait(ref, sem):
        pltpu.make_async_copy(ref, ref, sem).wait()

    def over_lvl(src, dst, send, recv):
        for k in range(1, n_lvl):
            peer = lvl_peer(k)
            copy(src(peer), dst, send, recv, (leaf, peer))

    def over_leaf(src, dst, send, recv):
        for k in range(1, n_leaf):
            peer = leaf_peer(k)
            copy(src(peer), dst, send, recv, (peer, lvl))

    barrier = pltpu.get_barrier_semaphore()
    for k in range(1, n_lvl):
        pl.semaphore_signal(barrier, inc=1, device_id=(leaf, lvl_peer(k)), device_id_type=MESH)
    for k in range(1, n_leaf):
        pl.semaphore_signal(barrier, inc=1, device_id=(leaf_peer(k), lvl), device_id_type=MESH)
    pl.semaphore_signal(barrier, inc=1, device_id=after_id, device_id_type=MESH)
    pl.semaphore_signal(barrier, inc=1, device_id=before_id, device_id_type=MESH)

    lane = iota((8, LANES), 1)
    low = lane < LANES // 2
    row8 = iota((8, LANES), 0)
    ranks = anchors_one.shape[2]
    own_one = jnp.concatenate([anchors_one[0], anchors_one[0]], axis=1)
    own_two = jnp.concatenate([anchors_two[0], anchors_two[0]], axis=1)
    partner = jnp.full((8, LANES), -1.0, F32)
    for k in range(far_one.shape[1]):
        value = lax.rem(far_one[0, k], n_lvl).astype(F32)
        partner = jnp.where(row8 == k, value, partner)
    s_anch[0] = own_one
    s_anch[1] = partner
    r_anch[lvl] = s_anch[...]
    s_top[...] = own_two
    r_top[leaf] = own_two

    n_dev = n_leaf * n_lvl
    tp = tree_pos[...]
    dest = lax.div(tp, pts)
    place = lax.rem(dest, n_lvl) * n_leaf + lax.div(dest, n_lvl)
    hit = iota((n_dev, pts), 0) == place
    hit16 = hit.astype(F32).astype(BF16)
    earlier = (iota((pts, pts), 0) < iota((pts, pts), 1)).astype(F32).astype(BF16)
    seen = dot(hit16, earlier)
    oh_user[:, :pts] = jnp.where(hit & (seen < 0.5), 1.0, 0.0).astype(BF16)
    oh_user[:, pts:] = jnp.where(hit & (seen > 0.5), 1.0, 0.0).astype(BF16)
    s_a[:, 0] = pack(oh_user[...], targets[...]).reshape(n_lvl, n_leaf, LANES)
    pos = jnp.broadcast_to(lax.rem(tp, pts).astype(F32), (rows, pts))
    s_a[:, 1] = pack(oh_user[...], pos).reshape(n_lvl, n_leaf, LANES)
    r_a[lvl] = s_a[lvl]

    pl.semaphore_wait(barrier, n_lvl + n_leaf)

    over_lvl(lambda p: s_a.at[p], r_a.at[lvl], set_send.at[0], set_recv.at[0])
    copy(coords, r_coords.at[0], set_send.at[1], set_recv.at[1], after_id)
    copy(coords, r_coords.at[1], set_send.at[2], set_recv.at[2], before_id)
    over_lvl(lambda p: s_anch, r_anch.at[lvl], set_send.at[3], set_recv.at[3])
    over_leaf(lambda p: s_top, r_top.at[leaf], set_send.at[4], set_recv.at[4])

    bt = jnp.concatenate(
        [dot_precise(jnp.transpose(transfer_one[c]), ubasis[c]) for c in range(clusters)], axis=1
    )
    b2t = dot_precise(jnp.transpose(transfer_two[0]), bt)
    ct = jnp.concatenate([bt, b2t], axis=0)
    ct_hi[...], ct_lo[...] = split2(ct)
    c_hi[...], c_lo[...] = split2(jnp.transpose(ct))

    wait(r_a.at[pl.ds(0, n_lvl - 1)], set_recv.at[0])
    for kind in range(2):
        s_b[:, kind] = jnp.swapaxes(r_a[:, kind], 0, 1)
    r_b[leaf] = s_b[leaf]
    over_leaf(lambda p: s_b.at[p], r_b.at[leaf], set_send.at[5], set_recv.at[5])

    wait(r_coords.at[0], set_recv.at[1])
    wait(r_coords.at[1], set_recv.at[2])
    src, dst = augmented(coords[...])
    src_pts[pts : 2 * pts] = jnp.transpose(src).astype(BF16)
    src_pts[:pts] = jnp.transpose(augmented(r_coords[0])[0]).astype(BF16)
    src_pts[2 * pts :] = jnp.transpose(augmented(r_coords[1])[0]).astype(BF16)
    dst = dst.astype(BF16)
    first = ring * clusters - clusters
    near_scale = (points * (near_lists + 1)) ** (-0.5)

    def near_rows(n, carry):
        at = pl.ds(pl.multiple_of(n * points, points), points)
        value = jnp.exp(dot(src_pts[at, :], dst))
        parts = []
        for c in range(clusters):
            weight = (n == c + clusters).astype(jnp.int32)
            for k in range(near_lists):
                rel = lax.rem(near_list[c, k] - first + total, total)
                weight = weight + (rel == n).astype(jnp.int32)
            scaled = weight.astype(F32) * near_scale
            parts.append(value[:, c * points : (c + 1) * points] * scaled)
        hi, lo = split2(jnp.concatenate(parts, axis=1))
        w_hi[at, :] = hi
        w_lo[at, :] = lo
        return carry

    lax.fori_loop(0, 3 * clusters, near_rows, 0)

    def lanes_of(get):
        tiles = []
        for m in range(n_lvl // 2):
            tiles.append(jnp.where(low, get(2 * m), get(2 * m + 1)))
        return jnp.concatenate(tiles, axis=1)

    wait(r_anch.at[pl.ds(0, n_lvl - 1)], set_recv.at[3])
    src, dst = augmented(lanes_of(lambda p: r_anch[p, 0]))
    wide = n_lvl * ranks
    partners = lanes_of(lambda p: r_anch[p, 1])
    owner = lax.div(iota((wide, wide), 0), ranks).astype(F32)
    count = jnp.zeros((wide, wide), F32)
    for k in range(far_one.shape[1]):
        count = count + jnp.where(owner == partners[k : k + 1], 1.0, 0.0)
    value = jnp.exp(dot(jnp.transpose(src).astype(BF16), dst.astype(BF16)))
    k1_hi[...], k1_lo[...] = split2(value * count * (far_one.shape[1] ** (-0.5)))

    def chosen(get):
        picks = []
        for k in range(far_two.shape[1]):
            which = far_two[0, k]
            value = get(0)
            for q in range(1, n_leaf):
                value = jnp.where(which == q, get(q), value)
            picks.append(value)
        return picks

    wait(r_top.at[pl.ds(0, n_leaf - 1)], set_recv.at[4])
    tops = chosen(lambda q: r_top[q])
    src, _ = augmented(
        jnp.concatenate([jnp.where(low, tops[m], tops[m + 1]) for m in (0, 2)], axis=1)
    )
    _, dst = augmented(own_two)
    value = jnp.exp(dot(jnp.transpose(src).astype(BF16), dst.astype(BF16)))
    value = jnp.where(iota(value.shape, 1) < LANES // 2, 0.0, value)
    k2_hi[...], k2_lo[...] = split2(value * (far_two.shape[1] ** (-0.5)))

    wait(r_b.at[pl.ds(0, n_leaf - 1)], set_recv.at[5])
    got_pos = r_b[:, 1].reshape(n_dev, LANES).astype(jnp.int32)
    column = iota((n_dev, pts), 1)
    oh_tree[:, :pts] = jnp.where(column == got_pos[:, 0:1], 1.0, 0.0).astype(BF16)
    half = LANES // 2
    oh_tree[:, pts:] = jnp.where(column == got_pos[:, half : half + 1], 1.0, 0.0).astype(BF16)
    vbuf[0] = unpack(oh_tree[...], r_b[:, 0].reshape(n_dev, LANES))
    pbuf[...] = jnp.zeros_like(pbuf)

    def apply(i, carry):
        copy(vbuf.at[i], r_halo.at[i, 0], send_sem.at[i, 0], halo_sem.at[i, 0], after_id)
        copy(vbuf.at[i], r_halo.at[i, 1], send_sem.at[i, 1], halo_sem.at[i, 1], before_id)
        v = vbuf[i]
        tu = dot_split(v, c_hi[...], c_lo[...])
        p = pbuf[...]
        q1 = jnp.sum(p * p, axis=1, keepdims=True)
        q2 = jnp.sum(v * v, axis=1, keepdims=True)
        sums = jnp.where(iota((rows, LANES), 1) < LANES // 4, q1, q2)
        s1[i, :, 0] = tu.reshape(n_lvl, 8, LANES)
        s1[i, :, 1] = sums.reshape(n_lvl, 8, LANES)
        r1[i, lvl] = s1[i, lvl]
        over_lvl(lambda peer: s1.at[i, peer], r1.at[i, lvl], send_sem.at[i, 2], stage_sem.at[i, 0])
        acc[...] = dot_split(v, w_hi[pts : 2 * pts], w_lo[pts : 2 * pts])

        wait(r1.at[i, pl.ds(0, n_lvl - 1)], stage_sem.at[i, 0])
        got = r1[i]
        up = jnp.sum(got[:, 0], axis=0)
        part_sums = jnp.sum(got[:, 1], axis=0)
        message = jnp.where(low, part_sums, up)
        s2[i] = message
        r2[i, leaf] = message
        over_leaf(lambda peer: s2.at[i], r2.at[i, leaf], send_sem.at[i, 3], stage_sem.at[i, 1])

        tiles = [
            jnp.where(low, got[2 * m, 0], pltpu.roll(got[2 * m + 1, 0], half, 1))
            for m in range(n_lvl // 2)
        ]
        f1 = dot_split(jnp.concatenate(tiles, axis=1), k1_hi[...], k1_lo[...])
        wait(r_halo.at[i, 0], halo_sem.at[i, 0])
        near = acc[...] + dot_split(r_halo[i, 0], w_hi[:pts], w_lo[:pts])
        wait(r_halo.at[i, 1], halo_sem.at[i, 1])
        acc[...] = near + dot_split(r_halo[i, 1], w_hi[2 * pts :], w_lo[2 * pts :])

        wait(r2.at[i, pl.ds(0, n_leaf - 1)], stage_sem.at[i, 1])
        all_sums = jnp.sum(r2[i], axis=0)
        ups = chosen(lambda q: r2[i, q])
        tiles = [jnp.where(low, pltpu.roll(ups[m], half, 1), ups[m + 1]) for m in (0, 2)]
        f2 = dot_split(jnp.concatenate(tiles, axis=1), k2_hi[...], k2_lo[...])
        for d in range(n_lvl):
            tile = f1[:, (d // 2) * LANES : (d // 2 + 1) * LANES]
            if d % 2:
                tile = pltpu.roll(tile, half, 1)
            s3[i, d, 0] = jnp.where(low, tile, f2)
            s3[i, d, 1] = all_sums
        r3[i, lvl] = s3[i, lvl]
        over_lvl(lambda peer: s3.at[i, peer], r3.at[i, lvl], send_sem.at[i, 4], stage_sem.at[i, 2])
        wait(r3.at[i, pl.ds(0, n_lvl - 1)], stage_sem.at[i, 2])
        pots = r3[i, :, 0].reshape(rows, LANES)
        sums = r3[i, :, 1].reshape(rows, LANES)
        sum_p = sums[:, 0:1]
        sum_v = sums[:, LANES // 4 : LANES // 4 + 1]
        out = acc[...] + dot_split(pots, ct_hi[...], ct_lo[...])

        @pl.when(i < 2)
        def _():
            vbuf[i + 1] = out

        @pl.when(i == 0)
        def _():
            pbuf[...] = out

        @pl.when(i == 2)
        def _():
            step = sum_p / (sum_p + sum_v + EPSILON)
            norm_ref[0] = jnp.broadcast_to(sum_p, (rows, LANES))
            step_ref[...] = jnp.broadcast_to(step, (rows, LANES))
            d0 = vbuf[1]
            vbuf[3] = d0 - step * (out + RIDGE * d0)

        @pl.when(i == 3)
        def _():
            beta = sum_v / (norm_ref[0][:, 0:1] + EPSILON)
            norm_ref[1] = jnp.broadcast_to(sum_v, (rows, LANES))
            pbuf[...] = vbuf[3] + beta * vbuf[1]
            vbuf[4] = out + beta * vbuf[2]

        @pl.when(i == 4)
        def _():
            step = norm_ref[1][:, 0:1] / (sum_p + sum_v + EPSILON)
            d1 = pbuf[...]
            sol = step_ref[...][:, 0:1] * vbuf[1] + step * d1
            res = vbuf[3] - step * (out + RIDGE * d1)
            s_c[:, 0] = pack(oh_tree[...], sol).reshape(n_leaf, n_lvl, LANES)
            s_c[:, 1] = pack(oh_tree[...], res).reshape(n_leaf, n_lvl, LANES)

        wait(vbuf.at[i], send_sem.at[i, 0])
        wait(vbuf.at[i], send_sem.at[i, 1])
        wait(r1.at[i, pl.ds(0, n_lvl - 1)], send_sem.at[i, 2])
        wait(r2.at[i, pl.ds(0, n_leaf - 1)], send_sem.at[i, 3])
        wait(r3.at[i, pl.ds(0, n_lvl - 1)], send_sem.at[i, 4])
        return carry

    lax.fori_loop(0, APPLIES, apply, 0)

    r_c[leaf] = s_c[leaf]
    over_leaf(lambda p: s_c.at[p], r_c.at[leaf], set_send.at[6], set_recv.at[6])
    wait(r_c.at[pl.ds(0, n_leaf - 1)], set_recv.at[6])
    for kind in range(2):
        s_d[:, kind] = jnp.swapaxes(r_c[:, kind], 0, 1)
    r_d[lvl] = s_d[lvl]
    over_lvl(lambda p: s_d.at[p], r_d.at[lvl], set_send.at[7], set_recv.at[7])
    wait(r_d.at[pl.ds(0, n_lvl - 1)], set_recv.at[7])
    coeffs[...] = unpack(oh_user[...], r_d[:, 0].reshape(n_dev, LANES))
    residual[...] = unpack(oh_user[...], r_d[:, 1].reshape(n_dev, LANES))

    wait(r_a.at[pl.ds(0, n_lvl - 1)], set_send.at[0])
    wait(r_coords.at[0], set_send.at[1])
    wait(r_coords.at[1], set_send.at[2])
    wait(r_anch.at[pl.ds(0, n_lvl - 1)], set_send.at[3])
    wait(r_top.at[pl.ds(0, n_leaf - 1)], set_send.at[4])
    wait(r_b.at[pl.ds(0, n_leaf - 1)], set_send.at[5])
    wait(r_c.at[pl.ds(0, n_leaf - 1)], set_send.at[6])
    wait(r_d.at[pl.ds(0, n_lvl - 1)], set_send.at[7])


def on_device(
    targets, tree_pos, coords, ubasis, transfer_one, transfer_two, anchors_one, anchors_two,
    near_list, far_one, far_two,
):
    rows, pts = targets.shape
    n_leaf, n_lvl = lax.axis_size("leaf"), lax.axis_size("lvl")
    n_dev = n_leaf * n_lvl
    dim = coords.shape[0]
    vmem = pl.BlockSpec(memory_space=pltpu.VMEM)
    smem = pl.BlockSpec(memory_space=pltpu.SMEM)
    V = pltpu.VMEM
    wide = n_lvl * anchors_one.shape[2]
    deep = far_two.shape[1] * anchors_two.shape[2]
    scratch = [
        V((n_dev, 2 * pts), BF16), V((n_dev, 2 * pts), BF16),
        V((n_lvl, 2, n_leaf, LANES), F32), V((n_lvl, 2, n_leaf, LANES), F32),
        V((n_leaf, 2, n_lvl, LANES), F32), V((n_leaf, 2, n_lvl, LANES), F32),
        V((n_leaf, 2, n_lvl, LANES), F32), V((n_leaf, 2, n_lvl, LANES), F32),
        V((n_lvl, 2, n_leaf, LANES), F32), V((n_lvl, 2, n_leaf, LANES), F32),
        V((2, dim, pts), F32),
        V((2, 8, LANES), F32), V((n_lvl, 2, 8, LANES), F32),
        V((8, LANES), F32), V((n_leaf, 8, LANES), F32),
        V((3 * pts, 64), BF16),
        V((3 * pts, pts), BF16), V((3 * pts, pts), BF16),
        V((wide, wide), BF16), V((wide, wide), BF16),
        V((deep, LANES), BF16), V((deep, LANES), BF16),
        V((pts, LANES), BF16), V((pts, LANES), BF16),
        V((LANES, pts), BF16), V((LANES, pts), BF16),
        V((APPLIES, rows, pts), F32), V((rows, pts), F32), V((rows, pts), F32),
        V((APPLIES, 2, rows, pts), F32),
        V((APPLIES, n_lvl, 2, 8, LANES), F32), V((APPLIES, n_lvl, 2, 8, LANES), F32),
        V((APPLIES, 8, LANES), F32), V((APPLIES, n_leaf, 8, LANES), F32),
        V((APPLIES, n_lvl, 2, 8, LANES), F32), V((APPLIES, n_lvl, 2, 8, LANES), F32),
        V((rows, LANES), F32), V((2, rows, LANES), F32),
        pltpu.SemaphoreType.DMA((8,)), pltpu.SemaphoreType.DMA((8,)),
        pltpu.SemaphoreType.DMA((APPLIES, 5)), pltpu.SemaphoreType.DMA((APPLIES, 2)),
        pltpu.SemaphoreType.DMA((APPLIES, 3)),
    ]
    out = jax.ShapeDtypeStruct((rows, pts), F32)
    body = lambda *refs: kernel((n_leaf, n_lvl), *refs)
    return pl.pallas_call(
        body,
        out_shape=(out, out),
        in_specs=[vmem] * 8 + [smem] * 3,
        out_specs=(vmem, vmem),
        scratch_shapes=scratch,
        compiler_params=pltpu.CompilerParams(
            collective_id=0, has_side_effects=True, vmem_limit_bytes=48 * 1024 * 1024
        ),
    )(
        targets, tree_pos.reshape(1, pts), coords, ubasis, transfer_one, transfer_two,
        anchors_one, anchors_two, near_list, far_one, far_two,
    )


def solution(mesh):
    both = ("leaf", "lvl")
    return jax.shard_map(
        on_device,
        mesh=mesh,
        in_specs=(
            P(None, both), P(both), P(None, both), P(both, None, None), P(both, None, None),
            P(both, None, None), P(both, None, None), P("leaf", None, None),
            P(both, None), P(both, None), P("leaf", None),
        ),
        out_specs=(P(None, both), P(None, both)),
        check_vma=False,
    )
```

time: 985 us -> 135 us (0.14)
  blocking collectives: 679 us -> 0 us
  Pallas kernels: 0 us -> 125 us
  starting transfers between devices: 97.4 us -> 0 us
  local copies, waits for them, and re-layouts: 87.3 us -> 8.89 us
  matrix products: 46.3 us -> 0 us
  waiting for transfers between devices: 33.2 us -> 0 us
  between operations: 18.3 us -> 0.67 us
  other arithmetic: 13.4 us -> 0 us
    psum x8 -> x0, blocking collectives: 352 us -> none  [the longest x2 162 us: residual_norm(): return lax.psum(jnp.sum(resid_vec * resid_vec, axis=1), ('leaf', 'lvl'))]
    all_gather x12 -> x0, blocking collectives: 327 us -> none  [the longest x5 187 us: apply_operator(): upper_all = lax.all_gather(upper_skel[None], 'leaf', axis=0, tiled=True)]
    pallas_call x0 -> x1, Pallas kernels: none -> 125 us  [on_device(): pl.pallas_call(body, out_shape=(out, out), in_specs=[vmem] * 8 + [smem] *...]
    ppermute x12 -> x0, starting transfers between devices: 50.7 us -> none  [the longest x6 45.5 us: with_halo(): after = lax.ppermute(leading, axis, down)]
    gather x48 -> x0, local copies, waits for them, and re-layouts: 48.7 us -> none  [the longest x35 37.2 us: apply_operator(): partner_vals = jnp.take(ext_blocks, rel_index[:, column], axis=1)]
    all_to_all x8 -> x0, starting transfers between devices: 46.7 us -> none  [the longest x1 10.6 us: on_device(): lax.all_to_all(send_pos, 'leaf', split_axis=1, concat_axis=1, tiled=True)]
    dot_general x120 -> x0, matrix products: 46.3 us -> none  [the longest x35 16.8 us: apply_operator(): jnp.einsum('rcq,cqp->rcp', partner_vals, blocks[column + 1], precision=PR...]
    all_to_all x8 -> x0, waiting for transfers between devices: 23.7 us -> none  [the longest x1 8.23 us: on_device(): lax.all_to_all(back_res, 'leaf', split_axis=1, concat_axis=1, tiled=True)]
  transfers between devices with their start and end apart: 20 -> 0, of which waited for: 9 -> 0; matrix products, arithmetic and copies ran while one was open for 5% -> 0% of each run, Pallas kernels for 0% -> 0%
where the time goes in v1:
time: 135 us; the launch traced here: 134 us
  Pallas kernels  125 us (93%)
  local copies, waits for them, and re-layouts  8.89 us (7%)
    pallas_call x1, Pallas kernels, on_device(): pl.pallas_call(body, out_shape=(out, out), in_specs=[vmem] * 8 + [smem] *...  125 us
    unnamed x24, local copies, waits for them, and re-layouts  8.89 us

profile of v1, /device:TPU:1, one launch (start us, length us, event | category | flops | bytes accessed | tf_op | source)
XLA Modules:
  0.0 134.1 jit_solution(5210723864334938335)
XLA Ops:
  0.6 0.0 copy-start.10
  0.6 0.0 copy-start.9
  0.7 0.6 copy-done.10
  1.3 0.0 copy-done.9
  1.3 0.0 copy-start
  1.3 0.9 copy-done
  2.2 0.0 copy-start.1
  2.2 0.9 copy-done.1
  3.1 0.0 copy-start.2
  3.1 0.9 copy-done.2
  4.0 0.0 copy-start.3
  4.0 0.8 copy-done.3
  4.8 0.0 copy-start.4
  4.8 0.7 copy-done.4
  5.5 0.0 copy-start.5
  5.5 0.7 copy-done.5
  6.2 0.0 copy-start.6
  6.2 0.7 copy-done.6
  6.9 0.0 copy-start.7
  6.9 0.7 copy-done.7
  7.6 0.0 copy-start.8
  7.6 0.7 copy-done.8
  8.2 124.6 %shard_map.122 = (f32[64,512]{1,0:T(8,128)S(1)}, f32[64,512]{1,0:T(8,128)S(1)}) custom-call(f32[64,512]{1,0:T(8,128)S(1)} %copy-done, s32[1,512]{1,0:T(1,128)S(1)} %bitcast.1, f32[8,512]{1,0:T(8,128)S(1)} %copy-done.4, f32[4,64,128]{2,1,0:T(8,128)S(1)} %copy-done.1, f32[4,64,64]{2,1,0:T(8,128)S(1)} %copy-done.2, f32[1,64,64]{2,1,0:T(8,128)S(1)} %copy-done.3, ...), custom_call_target="tpu_custom_call" | custom-call | tf_op jit(solution)/shard_map/pallas_call | solution.py:434
  132.8 0.7 copy.15
  133.5 0.7 copy.16
Async XLA Ops:
  0.6 0.7 copy-start.10
  0.6 0.7 copy-start.9
  1.3 0.9 copy-start
  2.2 0.9 copy-start.1
  3.1 0.9 copy-start.2
  4.0 0.8 copy-start.3
  4.8 0.7 copy-start.4
  5.5 0.7 copy-start.5
  6.2 0.7 copy-start.6
  6.9 0.7 copy-start.7
  7.6 0.7 copy-start.8

commit v2 on v1

v2 whole, which is shorter than its diff:
```python
import jax
import jax.numpy as jnp
from jax import lax
from jax.experimental import pallas as pl
from jax.experimental.pallas import tpu as pltpu
from jax.sharding import PartitionSpec as P

F32 = jnp.float32
BF16 = jnp.bfloat16
MESH = pl.DeviceIdType.MESH
PRECISE = lax.Precision.HIGHEST
DIM = 8
RIDGE = 1.0
EPSILON = 1e-6
APPLIES = 5
LANES = 128


def dot(a, b, ca=1, cb=0):
    return lax.dot_general(a, b, (((ca,), (cb,)), ((), ())), preferred_element_type=F32)


def dot_precise(a, b):
    return lax.dot_general(
        a, b, (((1,), (0,)), ((), ())), precision=PRECISE, preferred_element_type=F32
    )


def split2(x):
    hi = x.astype(BF16)
    return hi, (x - hi.astype(F32)).astype(BF16)


def split3(x):
    hi = x.astype(BF16)
    rest = x - hi.astype(F32)
    mid = rest.astype(BF16)
    return hi, mid, (rest - mid.astype(F32)).astype(BF16)


def dot_split(a, b_hi, b_lo):
    rows = a.shape[0]
    a_hi, a_lo = split2(a)
    both = dot(jnp.concatenate([a_hi, a_lo], axis=0), b_hi)
    return both[:rows] + both[rows:] + dot(a_hi, b_lo)


def iota(shape, dim):
    return lax.broadcasted_iota(jnp.int32, shape, dim)


def augmented(x):
    n = x.shape[1]
    x1, x2, x3 = (p.astype(F32) for p in split3(x))
    sq = jnp.sum(x * x, axis=0, keepdims=True) * (-1.0 / DIM)
    n1, n2, n3 = (p.astype(F32) for p in split3(sq))
    row = iota((8, n), 0)
    lead = jnp.where(row == 0, n1, jnp.where(row == 1, n2, n3))
    tail = jnp.where(row == 3, n1, jnp.where(row == 4, n2, n3))
    zero = jnp.zeros((8, n), F32)
    src_norm = jnp.where(row < 3, lead, jnp.where(row < 6, 1.0, 0.0))
    dst_norm = jnp.where(row < 3, 1.0, jnp.where(row < 6, tail, 0.0))
    q = 2.0 / DIM
    src = jnp.concatenate([x1, x1, x2, x1, x3, x2, src_norm, zero], axis=0)
    dst = jnp.concatenate([x1 * q, x2 * q, x1 * q, x3 * q, x1 * q, x2 * q, dst_norm, zero], axis=0)
    return src, dst


def pack(onehot, x):
    total = None
    for part in split3(x):
        zero = jnp.zeros_like(part)
        wide = jnp.concatenate(
            [jnp.concatenate([part, zero], axis=1), jnp.concatenate([zero, part], axis=1)], axis=0
        )
        term = dot(onehot, wide, 1, 1)
        total = term if total is None else total + term
    return total


def unpack(onehot, g):
    half = g.shape[1] // 2
    cols = onehot.shape[1] // 2
    gt = jnp.transpose(g)
    total = None
    for part in split3(gt):
        term = dot(part, onehot)
        total = term if total is None else total + term
    return total[:half, :cols] + total[half:, cols:]


def kernel(
    sizes,
    targets_h, tree_pos_h, coords_h, ubasis_h, transfer_one_h, transfer_two_h, anchors_one_h,
    anchors_two_h, near_list, far_one, far_two,
    coeffs, residual,
    targets, tree_pos, coords, ubasis, transfer_one, transfer_two, anchors_one, anchors_two,
    oh_user, oh_tree, s_a, r_a, s_b, r_b, s_c, r_c, s_d, r_d,
    r_coords, s_anch, r_anch, s_top, r_top, s_g, r_g, ct_full, r_ct,
    src_pts, w_hi, w_lo, k1_hi, k1_lo, k2_hi, k2_lo, c_hi, c_lo, ct_hi, ct_lo, m_hi, m_lo,
    tg_hi, tg_lo,
    wbuf, acc, r_halo, qbuf, s1, r1, s2, r2, s3, r3,
    in_sem, set_send, set_recv, halo_send, halo_recv, send1, recv1, send2, recv2, send3, recv3,
):
    n_leaf, n_lvl = sizes
    n_dev = n_leaf * n_lvl
    leaf, lvl = lax.axis_index("leaf"), lax.axis_index("lvl")
    rows, pts = targets.shape
    clusters = ubasis.shape[0]
    points = ubasis.shape[2]
    ranks = ubasis.shape[1]
    half = LANES // 2
    total = n_dev * clusters
    near_lists = near_list.shape[1]
    lower_count = far_one.shape[1]
    upper_count = far_two.shape[1]

    inputs = []
    pairs = (
        (tree_pos_h, tree_pos), (targets_h, targets), (transfer_one_h, transfer_one),
        (ubasis_h, ubasis), (transfer_two_h, transfer_two), (coords_h, coords),
        (anchors_one_h, anchors_one), (anchors_two_h, anchors_two),
    )
    for k, (hbm, vmem) in enumerate(pairs):
        inputs.append(pltpu.make_async_copy(hbm, vmem, in_sem.at[k]))
        inputs[-1].start()

    def lvl_peer(k):
        return lax.rem(lvl + k, n_lvl)

    def leaf_peer(k):
        return lax.rem(leaf + k, n_leaf)

    ring = leaf * n_lvl + lvl
    after = lax.rem(ring + 1, n_dev)
    before = lax.rem(ring + n_dev - 1, n_dev)
    after_id = (after // n_lvl, lax.rem(after, n_lvl))
    before_id = (before // n_lvl, lax.rem(before, n_lvl))

    def copy(src, dst, send, recv, device):
        pltpu.make_async_remote_copy(
            src_ref=src, dst_ref=dst, send_sem=send, recv_sem=recv,
            device_id=device, device_id_type=MESH,
        ).start()

    def wait(ref, sem):
        pltpu.make_async_copy(ref, ref, sem).wait()

    def over_lvl(src, dst, send, recv):
        for k in range(1, n_lvl):
            peer = lvl_peer(k)
            copy(src(peer), dst, send, recv, (leaf, peer))

    def over_leaf(src, dst, send, recv):
        for k in range(1, n_leaf):
            peer = leaf_peer(k)
            copy(src(peer), dst, send, recv, (peer, lvl))

    barrier = pltpu.get_barrier_semaphore()
    for k in range(1, n_leaf):
        pl.semaphore_signal(barrier, inc=1, device_id=(leaf_peer(k), lvl), device_id_type=MESH)
    for k in range(1, n_lvl):
        pl.semaphore_signal(barrier, inc=1, device_id=(leaf, lvl_peer(k)), device_id_type=MESH)
    pl.semaphore_signal(barrier, inc=1, device_id=after_id, device_id_type=MESH)
    pl.semaphore_signal(barrier, inc=1, device_id=before_id, device_id_type=MESH)

    lane = iota((8, LANES), 1)
    low = lane < half
    row8 = iota((8, LANES), 0)
    low_rows = iota((rows, LANES), 1) < half

    inputs[0].wait()
    tp = tree_pos[...]
    dest = lax.div(tp, pts)
    place = lax.rem(dest, n_lvl) * n_leaf + lax.div(dest, n_lvl)
    hit = iota((n_dev, pts), 0) == place
    hit16 = hit.astype(F32).astype(BF16)
    earlier = (iota((pts, pts), 0) < iota((pts, pts), 1)).astype(F32).astype(BF16)
    seen = dot(hit16, earlier)
    oh_user[:, :pts] = jnp.where(hit & (seen < 0.5), 1.0, 0.0).astype(BF16)
    oh_user[:, pts:] = jnp.where(hit & (seen > 0.5), 1.0, 0.0).astype(BF16)
    inputs[1].wait()
    s_a[:, 0] = pack(oh_user[...], targets[...]).reshape(n_lvl, n_leaf, LANES)
    pos = jnp.broadcast_to(lax.rem(tp, pts).astype(F32), (rows, pts))
    s_a[:, 1] = pack(oh_user[...], pos).reshape(n_lvl, n_leaf, LANES)
    r_a[lvl] = s_a[lvl]

    for k in range(2, len(pairs)):
        inputs[k].wait()
    own_one = jnp.concatenate([anchors_one[0], anchors_one[0]], axis=1)
    own_two = jnp.concatenate([anchors_two[0], anchors_two[0]], axis=1)
    partner = jnp.full((8, LANES), -1.0, F32)
    for k in range(lower_count):
        value = lax.rem(far_one[0, k], n_lvl).astype(F32)
        partner = jnp.where(row8 == k, value, partner)
    s_anch[0] = own_one
    s_anch[1] = partner
    r_anch[lvl] = s_anch[...]
    partner = jnp.full((8, LANES), -1.0, F32)
    for k in range(upper_count):
        partner = jnp.where(row8 == k, far_two[0, k].astype(F32), partner)
    s_top[0] = own_two
    s_top[1] = partner
    r_top[leaf] = s_top[...]

    pl.semaphore_wait(barrier, n_lvl + n_leaf)

    over_lvl(lambda p: s_a.at[p], r_a.at[lvl], set_send.at[0], set_recv.at[0])
    copy(coords, r_coords.at[0], set_send.at[1], set_recv.at[1], after_id)
    copy(coords, r_coords.at[1], set_send.at[2], set_recv.at[2], before_id)
    over_lvl(lambda p: s_anch, r_anch.at[lvl], set_send.at[3], set_recv.at[3])
    over_leaf(lambda p: s_top, r_top.at[leaf], set_send.at[4], set_recv.at[4])

    bt = jnp.concatenate(
        [dot_precise(jnp.transpose(transfer_one[c]), ubasis[c]) for c in range(clusters)], axis=1
    )
    b2t = dot_precise(jnp.transpose(transfer_two[0]), bt)
    ct = jnp.concatenate([bt, b2t], axis=0)
    c = jnp.transpose(ct)
    ct_full[...] = b2t
    ct_hi[...], ct_lo[...] = split2(ct)
    c_hi[...], c_lo[...] = split2(c)
    s_g[...] = dot_split(b2t, c_hi[...], c_lo[...])
    r_g[lvl] = s_g[...]

    wait(r_a.at[pl.ds(0, n_lvl - 1)], set_recv.at[0])
    for kind in range(2):
        s_b[:, kind] = jnp.swapaxes(r_a[:, kind], 0, 1)
    r_b[leaf] = s_b[leaf]
    over_leaf(lambda p: s_b.at[p], r_b.at[leaf], set_send.at[5], set_recv.at[5])
    over_lvl(lambda p: s_g, r_g.at[lvl], set_send.at[8], set_recv.at[8])
    copy(ct_full, r_ct.at[0], set_send.at[6], set_recv.at[6], after_id)
    copy(ct_full, r_ct.at[1], set_send.at[7], set_recv.at[7], before_id)

    wait(r_coords.at[0], set_recv.at[1])
    wait(r_coords.at[1], set_recv.at[2])
    src, dst = augmented(coords[...])
    src_pts[pts : 2 * pts] = jnp.transpose(src).astype(BF16)
    src_pts[:pts] = jnp.transpose(augmented(r_coords[0])[0]).astype(BF16)
    src_pts[2 * pts :] = jnp.transpose(augmented(r_coords[1])[0]).astype(BF16)
    dst = dst.astype(BF16)
    first = ring * clusters - clusters
    near_scale = (points * (near_lists + 1)) ** (-0.5)

    def near_rows(n, carry):
        at = pl.ds(pl.multiple_of(n * points, points), points)
        value = jnp.exp(dot(src_pts[at, :], dst))
        parts = []
        for c in range(clusters):
            weight = (n == c + clusters).astype(jnp.int32)
            for k in range(near_lists):
                rel = lax.rem(near_list[c, k] - first + total, total)
                weight = weight + (rel == n).astype(jnp.int32)
            scaled = weight.astype(F32) * near_scale
            parts.append(value[:, c * points : (c + 1) * points] * scaled)
        hi, lo = split2(jnp.concatenate(parts, axis=1))
        w_hi[at, :] = hi
        w_lo[at, :] = lo
        return carry

    lax.fori_loop(0, 3 * clusters, near_rows, 0)

    def lanes_of(get):
        tiles = []
        for m in range(n_lvl // 2):
            tiles.append(jnp.where(low, get(2 * m), get(2 * m + 1)))
        return jnp.concatenate(tiles, axis=1)

    wait(r_anch.at[pl.ds(0, n_lvl - 1)], set_recv.at[3])
    src, dst = augmented(lanes_of(lambda p: r_anch[p, 0]))
    wide = n_lvl * ranks
    partners = lanes_of(lambda p: r_anch[p, 1])
    owner = lax.div(iota((wide, wide), 0), ranks).astype(F32)
    count = jnp.zeros((wide, wide), F32)
    for k in range(lower_count):
        count = count + jnp.where(owner == partners[k : k + 1], 1.0, 0.0)
    value = jnp.exp(dot(jnp.transpose(src).astype(BF16), dst.astype(BF16)))
    k1_hi[...], k1_lo[...] = split2(value * count * (lower_count ** (-0.5)))

    wait(r_top.at[pl.ds(0, n_leaf - 1)], set_recv.at[4])
    groups = (leaf, leaf_peer(n_leaf - 1), leaf_peer(1))

    def chosen(lists, get):
        named = [jnp.broadcast_to(lists[k : k + 1], (8, LANES)) for k in range(upper_count)]
        picks = [get(0)] * upper_count
        for q in range(1, n_leaf):
            value = get(q)
            picks = [jnp.where(n == float(q), value, p) for n, p in zip(named, picks)]
        return picks

    for g, group in enumerate(groups):
        tops = chosen(r_top[group, 1], lambda q: r_top[q, 0])
        src, _ = augmented(
            jnp.concatenate([jnp.where(low, tops[m], tops[m + 1]) for m in (0, 2)], axis=1)
        )
        _, dst = augmented(r_top[group, 0])
        value = jnp.exp(dot(jnp.transpose(src).astype(BF16), dst.astype(BF16)))
        first_half = iota(value.shape, 1) < half
        value = jnp.where(first_half, 0.0, value) if g == 0 else jnp.where(first_half, value, 0.0)
        k2_hi[g], k2_lo[g] = split2(value * (upper_count ** (-0.5)))

    wait(r_g.at[pl.ds(0, n_lvl - 1)], set_recv.at[8])
    low_ranks = iota((ranks, LANES), 1) < half
    gamma = r_g[0]
    for p in range(1, n_lvl):
        gamma = gamma + r_g[p]
    tiles = [
        jnp.where(low_ranks, r_g[2 * m], pltpu.roll(r_g[2 * m + 1], half, 1))
        for m in range(n_lvl // 2)
    ]
    tiles.append(jnp.where(low_ranks, 0.0, gamma))
    tg = jnp.concatenate(tiles, axis=1)
    tg_hi[...], tg_lo[...] = split2(jnp.concatenate([jnp.zeros_like(tg), tg], axis=0))
    wait(r_ct.at[0], set_recv.at[6])
    wait(r_ct.at[1], set_recv.at[7])
    z_own = dot_split(ct_full[...], w_hi[pts : 2 * pts], w_lo[pts : 2 * pts])
    z_prev = dot_split(r_ct[0], w_hi[:pts], w_lo[:pts])
    z_next = dot_split(r_ct[1], w_hi[2 * pts :], w_lo[2 * pts :])
    at_first = (lvl == 0).astype(F32)
    at_last = (lvl == n_lvl - 1).astype(F32)
    z_main = z_own + z_prev * (1.0 - at_first) + z_next * (1.0 - at_last)
    z_edge = z_prev * at_first + z_next * at_last
    m_hi[...], m_lo[...] = split2(
        jnp.concatenate([bt, z_main, z_edge, jnp.zeros_like(z_edge)], axis=0)
    )

    wait(r_b.at[pl.ds(0, n_leaf - 1)], set_recv.at[5])
    got_pos = r_b[:, 1].reshape(n_dev, LANES).astype(jnp.int32)
    column = iota((n_dev, pts), 1)
    oh_tree[:, :pts] = jnp.where(column == got_pos[:, 0:1], 1.0, 0.0).astype(BF16)
    oh_tree[:, pts:] = jnp.where(column == got_pos[:, half : half + 1], 1.0, 0.0).astype(BF16)
    wbuf[0] = unpack(oh_tree[...], r_b[:, 0].reshape(n_dev, LANES))

    def send_halo(j):
        copy(wbuf.at[j], r_halo.at[j, 0], halo_send.at[j, 0], halo_recv.at[j, 0], after_id)
        copy(wbuf.at[j], r_halo.at[j, 1], halo_send.at[j, 1], halo_recv.at[j, 1], before_id)

    def scatter(j, value):
        s1[j] = value.reshape(n_lvl, 8, LANES)
        r1[j, lvl] = s1[j, lvl]
        over_lvl(lambda peer: s1.at[j, peer], r1.at[j, lvl], send1.at[j], recv1.at[j])

    def broadcast(j, value):
        s2[j] = value
        r2[j, leaf] = value
        over_leaf(lambda peer: s2.at[j], r2.at[j, leaf], send2.at[j], recv2.at[j])

    def gather(j):
        r3[j, lvl] = s3[j, lvl]
        over_lvl(lambda peer: s3.at[j, peer], r3.at[j, lvl], send3.at[j], recv3.at[j])

    def wait1(j):
        wait(r1.at[j, pl.ds(0, n_lvl - 1)], recv1.at[j])

    def wait2(j):
        wait(r2.at[j, pl.ds(0, n_leaf - 1)], recv2.at[j])

    def wait3(j):
        wait(r3.at[j, pl.ds(0, n_lvl - 1)], recv3.at[j])

    def send_potentials(j, f1, f2, edges):
        for d in range(n_lvl):
            tile = jnp.zeros((8, LANES), F32)
            if f1 is not None:
                tile = f1[:, (d // 2) * LANES : (d // 2 + 1) * LANES]
                if d % 2:
                    tile = pltpu.roll(tile, half, 1)
            s3[j, d, 0] = jnp.where(low, tile, f2)
            s3[j, d, 1] = edges[0] if d == 0 else edges[1] if d == n_lvl - 1 else jnp.zeros_like(f2)
        gather(j)

    def level_one(own, extra):
        tiles = [
            jnp.where(low, own[2 * m], pltpu.roll(own[2 * m + 1], half, 1))
            for m in range(n_lvl // 2)
        ]
        t = jnp.concatenate(tiles, axis=1)
        if extra is not None:
            t = t + extra
        return dot_split(t, k1_hi[...], k1_lo[...])

    def return_leaf(kind, value):
        s_c[kind] = pack(oh_tree[...], value).reshape(n_leaf, n_lvl, LANES)
        r_c[kind, leaf] = s_c[kind, leaf]
        over_leaf(
            lambda p: s_c.at[kind, p], r_c.at[kind, leaf], set_send.at[9 + kind], set_recv.at[9 + kind]
        )

    def return_lvl(kind):
        wait(r_c.at[kind, pl.ds(0, n_leaf - 1)], set_recv.at[9 + kind])
        s_d[kind] = jnp.swapaxes(r_c[kind], 0, 1)
        r_d[kind, lvl] = s_d[kind, lvl]
        over_lvl(
            lambda p: s_d.at[kind, p], r_d.at[kind, lvl], set_send.at[12 + kind], set_recv.at[12 + kind]
        )

    def returned(kind):
        wait(r_d.at[kind, pl.ds(0, n_lvl - 1)], set_recv.at[12 + kind])
        return unpack(oh_user[...], r_d[kind].reshape(n_dev, LANES))

    zero8 = jnp.zeros((8, LANES), F32)
    scatter(0, dot_split(wbuf[0], c_hi[...], c_lo[...]))
    send_halo(0)
    wait1(0)
    got = r1[0]
    broadcast(0, jnp.sum(got, axis=0))
    send_potentials(0, level_one(got, None), zero8, (zero8, zero8))

    def body(j, last):
        near = dot_split(wbuf[j], w_hi[pts : 2 * pts], w_lo[pts : 2 * pts])
        wait(r_halo.at[j, 0], halo_recv.at[j, 0])
        near = near + dot_split(r_halo[j, 0], w_hi[:pts], w_lo[:pts])
        wait(r_halo.at[j, 1], halo_recv.at[j, 1])
        acc[...] = near + dot_split(r_halo[j, 1], w_hi[2 * pts :], w_lo[2 * pts :])

        wait3(j)
        main = r3[j, :, 0].reshape(rows, LANES)
        edge = r3[j, :, 1].reshape(rows, LANES)
        moved = dot_split(jnp.concatenate([main, edge], axis=1), m_hi[...], m_lo[...])
        w_next = acc[...] + moved
        wbuf[j + 1] = w_next
        if not last:
            scatter(j + 1, dot_split(w_next, c_hi[...], c_lo[...]))
            send_halo(j + 1)
        power = wbuf[j] + dot_split(jnp.where(low_rows, 0.0, main), ct_hi[...], ct_lo[...])
        square = jnp.sum(power * power, axis=1, keepdims=True)
        if last:
            part = iota((rows, LANES), 1) // (LANES // 4)
            sums = jnp.where(part == 3, square, 0.0)
            for k in range(3):
                sums = jnp.where(part == k, qbuf[k + 1], sums)
            scatter(j + 1, sums)
            return_lvl(1)
        else:
            qbuf[j] = jnp.broadcast_to(square, (rows, LANES))

            @pl.when(j == 1)
            def _():
                return_leaf(0, power)

            @pl.when(j == 2)
            def _():
                return_lvl(0)

            @pl.when(j == 3)
            def _():
                return_leaf(1, power)

        wait2(j)
        potentials = []
        for g, group in enumerate(groups):
            ups = chosen(r_top[group, 1], lambda q: r2[j, q])
            tiles = [jnp.where(low, pltpu.roll(ups[m], half, 1), ups[m + 1]) for m in (0, 2)]
            potentials.append(dot_split(jnp.concatenate(tiles, axis=1), k2_hi[g], k2_lo[g]))
        f2, edges = potentials[0], potentials[1:]
        if last:
            send_potentials(j + 1, None, f2, edges)
            wait1(j + 1)
            broadcast(j + 1, jnp.sum(r1[j + 1], axis=0))
            return
        add = dot_split(f2, tg_hi[...], tg_lo[...])
        wait1(j + 1)
        got = r1[j + 1]
        broadcast(j + 1, jnp.sum(got, axis=0) + add[:, wide:])
        send_potentials(j + 1, level_one(got, add[:, :wide]), f2, edges)

    def step(j, carry):
        body(j, False)
        return carry

    lax.fori_loop(0, APPLIES - 1, step, 0)
    body(APPLIES - 1, True)

    wait3(APPLIES)
    main = r3[APPLIES, :, 0].reshape(rows, LANES)
    return_leaf(
        2, wbuf[APPLIES] + dot_split(jnp.where(low_rows, 0.0, main), ct_hi[...], ct_lo[...])
    )
    back1 = returned(0)
    back3 = returned(1)
    wait2(APPLIES)
    sums = jnp.sum(r2[APPLIES], axis=0)
    for d in range(n_lvl):
        s3[APPLIES + 1, d, 0] = sums
        s3[APPLIES + 1, d, 1] = sums
    gather(APPLIES + 1)
    return_lvl(2)

    wait3(APPLIES + 1)
    sums = r3[APPLIES + 1, :, 0].reshape(rows, LANES)
    g1, g2, g3, g4 = (sums[:, k * (LANES // 4) : k * (LANES // 4) + 1] for k in range(4))
    step0 = g1 / (g2 + RIDGE * g1 + EPSILON)
    keep = 1.0 - RIDGE * step0
    fresh = keep * keep * g1 - 2.0 * step0 * keep * g2 + step0 * step0 * g3
    lead = keep + fresh / (g1 + EPSILON)
    direction_sq = lead * lead * g1 - 2.0 * lead * step0 * g2 + step0 * step0 * g3
    image_sq = lead * lead * g2 - 2.0 * lead * step0 * g3 + step0 * step0 * g4
    step1 = fresh / (image_sq + RIDGE * direction_sq + EPSILON)
    coeffs[...] = (step0 + step1 * lead) * back1 - (step1 * step0) * back3
    partial = (keep - RIDGE * step1 * lead) * back1 - (
        step0 + step1 * (lead - RIDGE * step0)
    ) * back3
    residual[...] = partial + (step1 * step0) * returned(2)

    wait(r_a.at[pl.ds(0, n_lvl - 1)], set_send.at[0])
    wait(r_coords.at[0], set_send.at[1])
    wait(r_coords.at[1], set_send.at[2])
    wait(r_anch.at[pl.ds(0, n_lvl - 1)], set_send.at[3])
    wait(r_top.at[pl.ds(0, n_leaf - 1)], set_send.at[4])
    wait(r_b.at[pl.ds(0, n_leaf - 1)], set_send.at[5])
    wait(r_ct.at[0], set_send.at[6])
    wait(r_ct.at[1], set_send.at[7])
    wait(r_g.at[pl.ds(0, n_lvl - 1)], set_send.at[8])
    for kind in range(3):
        wait(r_c.at[kind, pl.ds(0, n_leaf - 1)], set_send.at[9 + kind])
        wait(r_d.at[kind, pl.ds(0, n_lvl - 1)], set_send.at[12 + kind])

    def sent(j, carry):
        wait(r1.at[j, pl.ds(0, n_lvl - 1)], send1.at[j])
        wait(r2.at[j, pl.ds(0, n_leaf - 1)], send2.at[j])
        return carry

    lax.fori_loop(0, APPLIES + 1, sent, 0)

    def sent_halo(j, carry):
        wait(wbuf.at[j], halo_send.at[j, 0])
        wait(wbuf.at[j], halo_send.at[j, 1])
        return carry

    lax.fori_loop(0, APPLIES, sent_halo, 0)

    def sent_last(j, carry):
        wait(r3.at[j, pl.ds(0, n_lvl - 1)], send3.at[j])
        return carry

    lax.fori_loop(0, APPLIES + 2, sent_last, 0)


def on_device(
    targets, tree_pos, coords, ubasis, transfer_one, transfer_two, anchors_one, anchors_two,
    near_list, far_one, far_two,
):
    rows, pts = targets.shape
    n_leaf, n_lvl = lax.axis_size("leaf"), lax.axis_size("lvl")
    n_dev = n_leaf * n_lvl
    dim = coords.shape[0]
    ranks = anchors_one.shape[2]
    hbm = pl.BlockSpec(memory_space=pl.ANY)
    vmem = pl.BlockSpec(memory_space=pltpu.VMEM)
    smem = pl.BlockSpec(memory_space=pltpu.SMEM)
    V = pltpu.VMEM
    D = pltpu.SemaphoreType.DMA
    wide = n_lvl * ranks
    deep = far_two.shape[1] * ranks
    arrays = (
        targets, tree_pos.reshape(1, pts), coords, ubasis, transfer_one, transfer_two,
        anchors_one, anchors_two,
    )
    scratch = [V(a.shape, a.dtype) for a in arrays] + [
        V((n_dev, 2 * pts), BF16), V((n_dev, 2 * pts), BF16),
        V((n_lvl, 2, n_leaf, LANES), F32), V((n_lvl, 2, n_leaf, LANES), F32),
        V((n_leaf, 2, n_lvl, LANES), F32), V((n_leaf, 2, n_lvl, LANES), F32),
        V((3, n_leaf, n_lvl, LANES), F32), V((3, n_leaf, n_lvl, LANES), F32),
        V((3, n_lvl, n_leaf, LANES), F32), V((3, n_lvl, n_leaf, LANES), F32),
        V((2, dim, pts), F32),
        V((2, 8, LANES), F32), V((n_lvl, 2, 8, LANES), F32),
        V((2, 8, LANES), F32), V((n_leaf, 2, 8, LANES), F32),
        V((ranks, LANES), F32), V((n_lvl, ranks, LANES), F32),
        V((ranks, pts), F32), V((2, ranks, pts), F32),
        V((3 * pts, 64), BF16),
        V((3 * pts, pts), BF16), V((3 * pts, pts), BF16),
        V((wide, wide), BF16), V((wide, wide), BF16),
        V((3, deep, LANES), BF16), V((3, deep, LANES), BF16),
        V((pts, LANES), BF16), V((pts, LANES), BF16),
        V((LANES, pts), BF16), V((LANES, pts), BF16),
        V((2 * LANES, pts), BF16), V((2 * LANES, pts), BF16),
        V((LANES, wide + LANES), BF16), V((LANES, wide + LANES), BF16),
        V((APPLIES + 1, rows, pts), F32), V((rows, pts), F32),
        V((APPLIES, 2, rows, pts), F32), V((APPLIES - 1, rows, LANES), F32),
        V((APPLIES + 1, n_lvl, 8, LANES), F32), V((APPLIES + 1, n_lvl, 8, LANES), F32),
        V((APPLIES + 1, 8, LANES), F32), V((APPLIES + 1, n_leaf, 8, LANES), F32),
        V((APPLIES + 2, n_lvl, 2, 8, LANES), F32), V((APPLIES + 2, n_lvl, 2, 8, LANES), F32),
        D((len(arrays),)), D((15,)), D((15,)),
        D((APPLIES, 2)), D((APPLIES, 2)),
        D((APPLIES + 1,)), D((APPLIES + 1,)), D((APPLIES + 1,)), D((APPLIES + 1,)),
        D((APPLIES + 2,)), D((APPLIES + 2,)),
    ]
    out = jax.ShapeDtypeStruct((rows, pts), F32)
    body = lambda *refs: kernel((n_leaf, n_lvl), *refs)
    return pl.pallas_call(
        body,
        out_shape=(out, out),
        in_specs=[hbm] * len(arrays) + [smem] * 3,
        out_specs=(vmem, vmem),
        scratch_shapes=scratch,
        compiler_params=pltpu.CompilerParams(
            collective_id=0, has_side_effects=True, vmem_limit_bytes=56 * 1024 * 1024
        ),
    )(*arrays, near_list, far_one, far_two)


def solution(mesh):
    both = ("leaf", "lvl")
    return jax.shard_map(
        on_device,
        mesh=mesh,
        in_specs=(
            P(None, both), P(both), P(None, both), P(both, None, None), P(both, None, None),
            P(both, None, None), P(both, None, None), P("leaf", None, None),
            P(both, None), P(both, None), P("leaf", None),
        ),
        out_specs=(P(None, both), P(None, both)),
        check_vma=False,
    )
```

time: 135 us -> 97.9 us (0.73)
  Pallas kernels: 125 us -> 94.8 us
  local copies, waits for them, and re-layouts: 8.89 us -> 2.26 us
    pallas_call x1, Pallas kernels: 125 us -> 94.8 us  [on_device(): pl.pallas_call(body, out_shape=(out, out), in_specs=[hbm] * len(arrays) +...]
    unnamed x24 -> x4, local copies, waits for them, and re-layouts: 8.89 us -> 2.26 us
where the time goes in v2:
time: 97.9 us; the launch traced here: 97.7 us
  Pallas kernels  94.8 us (97%)
  local copies, waits for them, and re-layouts  2.26 us (2%)
    pallas_call x1, Pallas kernels, on_device(): pl.pallas_call(body, out_shape=(out, out), in_specs=[hbm] * len(arrays) +...  94.8 us
    unnamed x4, local copies, waits for them, and re-layouts  2.26 us

profile of v2, /device:TPU:1, one launch (start us, length us, event | category | flops | bytes accessed | tf_op | source)
XLA Modules:
  0.0 97.7 jit_solution(17608901861176632366)
XLA Ops:
  0.6 94.8 %shard_map.122 = (f32[64,512]{1,0:T(8,128)}, f32[64,512]{1,0:T(8,128)}) custom-call(f32[64,512]{1,0:T(8,128)} %refs_0_.1, s32[1,512]{1,0:T(1,128)} %bitcast.1, f32[8,512]{1,0:T(8,128)} %refs_2_.1, f32[4,64,128]{2,1,0:T(8,128)} %refs_3_.1, f32[4,64,64]{2,1,0:T(8,128)} %refs_4_.1, f32[1,64,64]{2,1,0:T(8,128)} %refs_5_.1, f32[1,8,64]{2,1,0:T(8,128)} %refs_6_.1, ...), custom_call_target="tpu_custom_call" | custom-call | tf_op jit(solution)/shard_map/pallas_call | solution.py:590
  95.5 0.0 copy-start
  95.5 1.6 %copy.15 = f32[64,512]{1,0:T(8,128)} copy(f32[64,512]{1,0:T(8,128)} %get-tuple-element.4) | data formatting | bytes 262144
  97.1 0.0 copy-done
  97.1 0.7 copy.16
Async XLA Ops:
  95.5 1.6 %copy-start = (f32[64,512]{1,0:T(8,128)S(1)}, f32[64,512]{1,0:T(8,128)}, u32[]{:S(2)}) copy-start(f32[64,512]{1,0:T(8,128)} %get-tuple-element.5) | copy-start | bytes 393220

commit v3 on v2

--- a/solution.py
+++ b/solution.py
@@ -125,11 +125,20 @@
         inputs.append(pltpu.make_async_copy(hbm, vmem, in_sem.at[k]))
         inputs[-1].start()
 
-    def lvl_peer(k):
-        return lax.rem(lvl + k, n_lvl)
-
-    def leaf_peer(k):
-        return lax.rem(leaf + k, n_leaf)
+    chips_z, cores = 8, 2
+    chips_y, chips_x = n_leaf // chips_z, n_lvl // cores
+
+    def others(long, short):
+        pairs = [(a, b) for a in range(long) for b in range(short)][1:]
+        far = lambda p: min(p[0], long - p[0]) + min(p[1], short - p[1]) * (short > 2)
+        return sorted(pairs, key=lambda p: -far(p))
+
+    def shifted(index, short, long, a, b):
+        return lax.rem(index // short + a, long) * short + lax.rem(lax.rem(index, short) + b, short)
+
+    leaf_peers = [shifted(leaf, chips_z, chips_y, a, b) for a, b in others(chips_y, chips_z)]
+    lvl_peers = [shifted(lvl, cores, chips_x, a, b) for a, b in others(chips_x, cores)]
+    leaf_before, leaf_after = lax.rem(leaf + n_leaf - 1, n_leaf), lax.rem(leaf + 1, n_leaf)
 
     ring = leaf * n_lvl + lvl
     after = lax.rem(ring + 1, n_dev)
@@ -147,20 +156,18 @@
         pltpu.make_async_copy(ref, ref, sem).wait()
 
     def over_lvl(src, dst, send, recv):
-        for k in range(1, n_lvl):
-            peer = lvl_peer(k)
+        for peer in lvl_peers:
             copy(src(peer), dst, send, recv, (leaf, peer))
 
     def over_leaf(src, dst, send, recv):
-        for k in range(1, n_leaf):
-            peer = leaf_peer(k)
+        for peer in leaf_peers:
             copy(src(peer), dst, send, recv, (peer, lvl))
 
     barrier = pltpu.get_barrier_semaphore()
-    for k in range(1, n_leaf):
-        pl.semaphore_signal(barrier, inc=1, device_id=(leaf_peer(k), lvl), device_id_type=MESH)
-    for k in range(1, n_lvl):
-        pl.semaphore_signal(barrier, inc=1, device_id=(leaf, lvl_peer(k)), device_id_type=MESH)
+    for peer in leaf_peers:
+        pl.semaphore_signal(barrier, inc=1, device_id=(peer, lvl), device_id_type=MESH)
+    for peer in lvl_peers:
+        pl.semaphore_signal(barrier, inc=1, device_id=(leaf, peer), device_id_type=MESH)
     pl.semaphore_signal(barrier, inc=1, device_id=after_id, device_id_type=MESH)
     pl.semaphore_signal(barrier, inc=1, device_id=before_id, device_id_type=MESH)
 
@@ -196,12 +203,12 @@
     s_anch[0] = own_one
     s_anch[1] = partner
     r_anch[lvl] = s_anch[...]
-    partner = jnp.full((8, LANES), -1.0, F32)
+    partner = own_two
     for k in range(upper_count):
-        partner = jnp.where(row8 == k, far_two[0, k].astype(F32), partner)
-    s_top[0] = own_two
-    s_top[1] = partner
-    r_top[leaf] = s_top[...]
+        value = far_two[0, k].astype(F32)
+        partner = jnp.where(jnp.logical_and(row8 == k, jnp.logical_not(low)), value, partner)
+    s_top[...] = partner
+    r_top[leaf] = partner
 
     pl.semaphore_wait(barrier, n_lvl + n_leaf)
 
@@ -278,9 +285,10 @@
     k1_hi[...], k1_lo[...] = split2(value * count * (lower_count ** (-0.5)))
 
     wait(r_top.at[pl.ds(0, n_leaf - 1)], set_recv.at[4])
-    groups = (leaf, leaf_peer(n_leaf - 1), leaf_peer(1))
+    groups = (leaf, leaf_before, leaf_after)
 
     def chosen(lists, get):
+        lists = jnp.where(low, pltpu.roll(lists, half, 1), lists)
         named = [jnp.broadcast_to(lists[k : k + 1], (8, LANES)) for k in range(upper_count)]
         picks = [get(0)] * upper_count
         for q in range(1, n_leaf):
@@ -289,11 +297,14 @@
         return picks
 
     for g, group in enumerate(groups):
-        tops = chosen(r_top[group, 1], lambda q: r_top[q, 0])
+        tops = chosen(r_top[group], lambda q: r_top[q])
         src, _ = augmented(
-            jnp.concatenate([jnp.where(low, tops[m], tops[m + 1]) for m in (0, 2)], axis=1)
+            jnp.concatenate(
+                [jnp.where(low, tops[m], pltpu.roll(tops[m + 1], half, 1)) for m in (0, 2)], axis=1
+            )
         )
-        _, dst = augmented(r_top[group, 0])
+        mine = r_top[group]
+        _, dst = augmented(jnp.where(low, mine, pltpu.roll(mine, half, 1)))
         value = jnp.exp(dot(jnp.transpose(src).astype(BF16), dst.astype(BF16)))
         first_half = iota(value.shape, 1) < half
         value = jnp.where(first_half, 0.0, value) if g == 0 else jnp.where(first_half, value, 0.0)
@@ -449,7 +460,7 @@
         wait2(j)
         potentials = []
         for g, group in enumerate(groups):
-            ups = chosen(r_top[group, 1], lambda q: r2[j, q])
+            ups = chosen(r_top[group], lambda q: r2[j, q])
             tiles = [jnp.where(low, pltpu.roll(ups[m], half, 1), ups[m + 1]) for m in (0, 2)]
             potentials.append(dot_split(jnp.concatenate(tiles, axis=1), k2_hi[g], k2_lo[g]))
         f2, edges = potentials[0], potentials[1:]
@@ -461,8 +472,8 @@
         add = dot_split(f2, tg_hi[...], tg_lo[...])
         wait1(j + 1)
         got = r1[j + 1]
+        send_potentials(j + 1, level_one(got, add[:, :wide]), f2, edges)
         broadcast(j + 1, jnp.sum(got, axis=0) + add[:, wide:])
-        send_potentials(j + 1, level_one(got, add[:, :wide]), f2, edges)
 
     def step(j, carry):
         body(j, False)
@@ -564,7 +575,7 @@
         V((3, n_lvl, n_leaf, LANES), F32), V((3, n_lvl, n_leaf, LANES), F32),
         V((2, dim, pts), F32),
         V((2, 8, LANES), F32), V((n_lvl, 2, 8, LANES), F32),
-        V((2, 8, LANES), F32), V((n_leaf, 2, 8, LANES), F32),
+        V((8, LANES), F32), V((n_leaf, 8, LANES), F32),
         V((ranks, LANES), F32), V((n_lvl, ranks, LANES), F32),
         V((ranks, pts), F32), V((2, ranks, pts), F32),
         V((3 * pts, 64), BF16),
@@ -594,7 +605,7 @@
         out_specs=(vmem, vmem),
         scratch_shapes=scratch,
         compiler_params=pltpu.CompilerParams(
-            collective_id=0, has_side_effects=True, vmem_limit_bytes=56 * 1024 * 1024
+            collective_id=0, has_side_effects=True, vmem_limit_bytes=60 * 1024 * 1024
         ),
     )(*arrays, near_list, far_one, far_two)
 

time: 97.9 us -> 96.5 us (0.986)
  Pallas kernels: 94.8 us -> 93.5 us
    pallas_call x1, Pallas kernels: 94.8 us -> 93.5 us  [on_device(): pl.pallas_call(body, out_shape=(out, out), in_specs=[hbm] * len(arrays) +...]
where the time goes in v3:
time: 96.5 us; the launch traced here: 96.4 us
  Pallas kernels  93.5 us (97%)
  local copies, waits for them, and re-layouts  2.26 us (2%)
    pallas_call x1, Pallas kernels, on_device(): pl.pallas_call(body, out_shape=(out, out), in_specs=[hbm] * len(arrays) +...  93.5 us
    unnamed x4, local copies, waits for them, and re-layouts  2.26 us

profile of v3, /device:TPU:1, one launch (start us, length us, event | category | flops | bytes accessed | tf_op | source)
XLA Modules:
  0.0 96.4 jit_solution(11114916120908184574)
XLA Ops:
  0.6 93.5 %shard_map.122 = (f32[64,512]{1,0:T(8,128)}, f32[64,512]{1,0:T(8,128)}) custom-call(f32[64,512]{1,0:T(8,128)} %refs_0_.1, s32[1,512]{1,0:T(1,128)} %bitcast.1, f32[8,512]{1,0:T(8,128)} %refs_2_.1, f32[4,64,128]{2,1,0:T(8,128)} %refs_3_.1, f32[4,64,64]{2,1,0:T(8,128)} %refs_4_.1, f32[1,64,64]{2,1,0:T(8,128)} %refs_5_.1, f32[1,8,64]{2,1,0:T(8,128)} %refs_6_.1, ...), custom_call_target="tpu_custom_call" | custom-call | tf_op jit(solution)/shard_map/pallas_call | solution.py:601
  94.1 0.0 copy-start
  94.1 1.6 %copy.15 = f32[64,512]{1,0:T(8,128)} copy(f32[64,512]{1,0:T(8,128)} %get-tuple-element.4) | data formatting | bytes 262144
  95.7 0.0 copy-done
  95.7 0.7 copy.16
Async XLA Ops:
  94.1 1.6 %copy-start = (f32[64,512]{1,0:T(8,128)S(1)}, f32[64,512]{1,0:T(8,128)}, u32[]{:S(2)}) copy-start(f32[64,512]{1,0:T(8,128)} %get-tuple-element.5) | copy-start | bytes 393220

commit v4 on v3

--- a/solution.py
+++ b/solution.py
@@ -93,13 +93,13 @@
     sizes,
     targets_h, tree_pos_h, coords_h, ubasis_h, transfer_one_h, transfer_two_h, anchors_one_h,
     anchors_two_h, near_list, far_one, far_two,
-    coeffs, residual,
+    result,
     targets, tree_pos, coords, ubasis, transfer_one, transfer_two, anchors_one, anchors_two,
-    oh_user, oh_tree, s_a, r_a, s_b, r_b, s_c, r_c, s_d, r_d,
+    oh_user, oh_tree, s_a, r_a, s_b, r_b, s_c, r_c, s_d, r_d, s_e, r_e, s_f, r_f,
     r_coords, s_anch, r_anch, s_top, r_top, s_g, r_g, ct_full, r_ct,
-    src_pts, w_hi, w_lo, k1_hi, k1_lo, k2_hi, k2_lo, c_hi, c_lo, ct_hi, ct_lo, m_hi, m_lo,
+    src_pts, w_hi, w_lo, k1_hi, k1_lo, k2_hi, k2_lo, c_hi, c_lo, ct_hi, ct_lo, m_hi, m_lo, mc_hi, mc_lo,
     tg_hi, tg_lo,
-    wbuf, acc, r_halo, qbuf, s1, r1, s2, r2, s3, r3,
+    wbuf, acc, tu_near, r_halo, qbuf, s1, r1, s2, r2, s3, r3,
     in_sem, set_send, set_recv, halo_send, halo_recv, send1, recv1, send2, recv2, send3, recv3,
 ):
     n_leaf, n_lvl = sizes
@@ -187,9 +187,22 @@
     oh_user[:, :pts] = jnp.where(hit & (seen < 0.5), 1.0, 0.0).astype(BF16)
     oh_user[:, pts:] = jnp.where(hit & (seen > 0.5), 1.0, 0.0).astype(BF16)
     inputs[1].wait()
-    s_a[:, 0] = pack(oh_user[...], targets[...]).reshape(n_lvl, n_leaf, LANES)
-    pos = jnp.broadcast_to(lax.rem(tp, pts).astype(F32), (rows, pts))
-    s_a[:, 1] = pack(oh_user[...], pos).reshape(n_lvl, n_leaf, LANES)
+    blocks = n_leaf // 8
+    packed = pack(oh_user[...], targets[...])
+    s_a[:, :blocks] = packed.reshape(n_lvl, blocks, 8, LANES)
+    pos = lax.rem(tp, pts).astype(F32)
+    pos_hi = pos.astype(BF16).astype(F32)
+    row16 = iota((16, pts), 0)
+    terms = jnp.where(row16 == 0, pos_hi, jnp.where(row16 == 1, pos - pos_hi, 0.0)).astype(BF16)
+    tile = jnp.zeros((8, LANES), F32)
+    for h in range(2):
+        both = dot(terms, oh_user[:, h * pts : (h + 1) * pts], 1, 1)
+        line = both[0:1] + both[1:2]
+        for q in range(n_dev // LANES):
+            part = line[:, q * LANES : (q + 1) * LANES]
+            tile = jnp.where(row8 == 2 * h + q, part, tile)
+    for p in range(n_lvl):
+        s_a[p, blocks] = tile
     r_a[lvl] = s_a[lvl]
 
     for k in range(2, len(pairs)):
@@ -231,8 +244,18 @@
     r_g[lvl] = s_g[...]
 
     wait(r_a.at[pl.ds(0, n_lvl - 1)], set_recv.at[0])
-    for kind in range(2):
-        s_b[:, kind] = jnp.swapaxes(r_a[:, kind], 0, 1)
+    s_b[:, :n_lvl] = jnp.swapaxes(r_a[:, :blocks].reshape(n_lvl, n_leaf, LANES), 0, 1)
+    per_row = LANES // n_leaf
+    mine = []
+    for h in range(2):
+        line = jnp.where(lvl < per_row, r_a[:, blocks, 2 * h], r_a[:, blocks, 2 * h + 1])
+        turned = line
+        for k in range(1, per_row):
+            here = lax.rem(lvl, per_row) == k
+            turned = jnp.where(here, pltpu.roll(line, LANES - k * n_leaf, 1), turned)
+        mine.append(turned)
+    square = jnp.concatenate(mine + [jnp.zeros((LANES - 16, LANES), F32)], axis=0)
+    s_b[:, n_lvl : n_lvl + 1] = jnp.transpose(square)[:n_leaf].reshape(n_leaf, 1, LANES)
     r_b[leaf] = s_b[leaf]
     over_leaf(lambda p: s_b.at[p], r_b.at[leaf], set_send.at[5], set_recv.at[5])
     over_lvl(lambda p: s_g, r_g.at[lvl], set_send.at[8], set_recv.at[8])
@@ -331,16 +354,20 @@
     at_last = (lvl == n_lvl - 1).astype(F32)
     z_main = z_own + z_prev * (1.0 - at_first) + z_next * (1.0 - at_last)
     z_edge = z_prev * at_first + z_next * at_last
-    m_hi[...], m_lo[...] = split2(
-        jnp.concatenate([bt, z_main, z_edge, jnp.zeros_like(z_edge)], axis=0)
-    )
+    m = jnp.concatenate([bt, z_main, z_edge, jnp.zeros_like(z_edge)], axis=0)
+    m_hi[...], m_lo[...] = split2(m)
+    mc_hi[...], mc_lo[...] = split2(dot_split(m, c_hi[...], c_lo[...]))
 
     wait(r_b.at[pl.ds(0, n_leaf - 1)], set_recv.at[5])
-    got_pos = r_b[:, 1].reshape(n_dev, LANES).astype(jnp.int32)
-    column = iota((n_dev, pts), 1)
-    oh_tree[:, :pts] = jnp.where(column == got_pos[:, 0:1], 1.0, 0.0).astype(BF16)
-    oh_tree[:, pts:] = jnp.where(column == got_pos[:, half : half + 1], 1.0, 0.0).astype(BF16)
-    wbuf[0] = unpack(oh_tree[...], r_b[:, 0].reshape(n_dev, LANES))
+    column = iota((n_dev, pts), 1).astype(F32)
+    row3 = iota((n_leaf, n_lvl, LANES), 1)
+    lane3 = iota((n_leaf, n_lvl, LANES), 2)
+    line = jnp.broadcast_to(r_b[:, n_lvl : n_lvl + 1], (n_leaf, n_lvl, LANES))
+    for h in range(2):
+        got = jnp.where(lane3 == row3 + h * n_lvl, line, 0.0).reshape(n_dev, LANES)
+        got = jnp.sum(got, axis=1, keepdims=True)
+        oh_tree[:, h * pts : (h + 1) * pts] = jnp.where(column == got, 1.0, 0.0).astype(BF16)
+    wbuf[0] = unpack(oh_tree[...], r_b[:, :n_lvl].reshape(n_dev, LANES))
 
     def send_halo(j):
         copy(wbuf.at[j], r_halo.at[j, 0], halo_send.at[j, 0], halo_recv.at[j, 0], after_id)
@@ -390,49 +417,41 @@
             t = t + extra
         return dot_split(t, k1_hi[...], k1_lo[...])
 
-    def return_leaf(kind, value):
-        s_c[kind] = pack(oh_tree[...], value).reshape(n_leaf, n_lvl, LANES)
-        r_c[kind, leaf] = s_c[kind, leaf]
-        over_leaf(
-            lambda p: s_c.at[kind, p], r_c.at[kind, leaf], set_send.at[9 + kind], set_recv.at[9 + kind]
-        )
-
-    def return_lvl(kind):
-        wait(r_c.at[kind, pl.ds(0, n_leaf - 1)], set_recv.at[9 + kind])
-        s_d[kind] = jnp.swapaxes(r_c[kind], 0, 1)
-        r_d[kind, lvl] = s_d[kind, lvl]
-        over_lvl(
-            lambda p: s_d.at[kind, p], r_d.at[kind, lvl], set_send.at[12 + kind], set_recv.at[12 + kind]
-        )
-
-    def returned(kind):
-        wait(r_d.at[kind, pl.ds(0, n_lvl - 1)], set_recv.at[12 + kind])
-        return unpack(oh_user[...], r_d[kind].reshape(n_dev, LANES))
+    def packed_back(value):
+        return pack(oh_tree[...], value).reshape(n_leaf, n_lvl, LANES)
+
+    def unpacked(rows_back):
+        return unpack(oh_user[...], rows_back.reshape(n_dev, LANES))
 
     zero8 = jnp.zeros((8, LANES), F32)
     scatter(0, dot_split(wbuf[0], c_hi[...], c_lo[...]))
     send_halo(0)
+    acc[...] = dot_split(wbuf[0], w_hi[pts : 2 * pts], w_lo[pts : 2 * pts])
     wait1(0)
     got = r1[0]
     broadcast(0, jnp.sum(got, axis=0))
     send_potentials(0, level_one(got, None), zero8, (zero8, zero8))
 
     def body(j, last):
-        near = dot_split(wbuf[j], w_hi[pts : 2 * pts], w_lo[pts : 2 * pts])
         wait(r_halo.at[j, 0], halo_recv.at[j, 0])
-        near = near + dot_split(r_halo[j, 0], w_hi[:pts], w_lo[:pts])
+        near = acc[...] + dot_split(r_halo[j, 0], w_hi[:pts], w_lo[:pts])
         wait(r_halo.at[j, 1], halo_recv.at[j, 1])
-        acc[...] = near + dot_split(r_halo[j, 1], w_hi[2 * pts :], w_lo[2 * pts :])
+        near = near + dot_split(r_halo[j, 1], w_hi[2 * pts :], w_lo[2 * pts :])
+        acc[...] = near
+        if not last:
+            tu_near[...] = dot_split(near, c_hi[...], c_lo[...])
 
         wait3(j)
         main = r3[j, :, 0].reshape(rows, LANES)
         edge = r3[j, :, 1].reshape(rows, LANES)
-        moved = dot_split(jnp.concatenate([main, edge], axis=1), m_hi[...], m_lo[...])
-        w_next = acc[...] + moved
+        moved = jnp.concatenate([main, edge], axis=1)
+        if not last:
+            scatter(j + 1, tu_near[...] + dot_split(moved, mc_hi[...], mc_lo[...]))
+        w_next = acc[...] + dot_split(moved, m_hi[...], m_lo[...])
         wbuf[j + 1] = w_next
         if not last:
-            scatter(j + 1, dot_split(w_next, c_hi[...], c_lo[...]))
             send_halo(j + 1)
+            acc[...] = dot_split(w_next, w_hi[pts : 2 * pts], w_lo[pts : 2 * pts])
         power = wbuf[j] + dot_split(jnp.where(low_rows, 0.0, main), ct_hi[...], ct_lo[...])
         square = jnp.sum(power * power, axis=1, keepdims=True)
         if last:
@@ -441,21 +460,18 @@
             for k in range(3):
                 sums = jnp.where(part == k, qbuf[k + 1], sums)
             scatter(j + 1, sums)
-            return_lvl(1)
         else:
             qbuf[j] = jnp.broadcast_to(square, (rows, LANES))
 
             @pl.when(j == 1)
             def _():
-                return_leaf(0, power)
-
-            @pl.when(j == 2)
-            def _():
-                return_lvl(0)
+                s_c[:, 0] = packed_back(power)
 
             @pl.when(j == 3)
             def _():
-                return_leaf(1, power)
+                s_c[:, 1] = packed_back(power)
+                r_c[leaf] = s_c[leaf]
+                over_leaf(lambda p: s_c.at[p], r_c.at[leaf], set_send.at[9], set_recv.at[9])
 
         wait2(j)
         potentials = []
@@ -482,20 +498,32 @@
     lax.fori_loop(0, APPLIES - 1, step, 0)
     body(APPLIES - 1, True)
 
+    wait(r_c.at[pl.ds(0, n_leaf - 1)], set_recv.at[9])
+    for kind in range(2):
+        s_d[:, kind] = jnp.swapaxes(r_c[:, kind], 0, 1)
+    r_d[lvl] = s_d[lvl]
+    over_lvl(lambda p: s_d.at[p], r_d.at[lvl], set_send.at[10], set_recv.at[10])
+
     wait3(APPLIES)
     main = r3[APPLIES, :, 0].reshape(rows, LANES)
-    return_leaf(
-        2, wbuf[APPLIES] + dot_split(jnp.where(low_rows, 0.0, main), ct_hi[...], ct_lo[...])
+    s_e[...] = packed_back(
+        wbuf[APPLIES] + dot_split(jnp.where(low_rows, 0.0, main), ct_hi[...], ct_lo[...])
     )
-    back1 = returned(0)
-    back3 = returned(1)
+    r_e[leaf] = s_e[leaf]
+    over_leaf(lambda p: s_e.at[p], r_e.at[leaf], set_send.at[11], set_recv.at[11])
+    wait(r_d.at[pl.ds(0, n_lvl - 1)], set_recv.at[10])
+    back1 = unpacked(r_d[:, 0])
+    back3 = unpacked(r_d[:, 1])
     wait2(APPLIES)
     sums = jnp.sum(r2[APPLIES], axis=0)
     for d in range(n_lvl):
         s3[APPLIES + 1, d, 0] = sums
         s3[APPLIES + 1, d, 1] = sums
     gather(APPLIES + 1)
-    return_lvl(2)
+    wait(r_e.at[pl.ds(0, n_leaf - 1)], set_recv.at[11])
+    s_f[...] = jnp.swapaxes(r_e[...], 0, 1)
+    r_f[lvl] = s_f[lvl]
+    over_lvl(lambda p: s_f.at[p], r_f.at[lvl], set_send.at[12], set_recv.at[12])
 
     wait3(APPLIES + 1)
     sums = r3[APPLIES + 1, :, 0].reshape(rows, LANES)
@@ -507,11 +535,12 @@
     direction_sq = lead * lead * g1 - 2.0 * lead * step0 * g2 + step0 * step0 * g3
     image_sq = lead * lead * g2 - 2.0 * lead * step0 * g3 + step0 * step0 * g4
     step1 = fresh / (image_sq + RIDGE * direction_sq + EPSILON)
-    coeffs[...] = (step0 + step1 * lead) * back1 - (step1 * step0) * back3
+    result[0] = (step0 + step1 * lead) * back1 - (step1 * step0) * back3
     partial = (keep - RIDGE * step1 * lead) * back1 - (
         step0 + step1 * (lead - RIDGE * step0)
     ) * back3
-    residual[...] = partial + (step1 * step0) * returned(2)
+    wait(r_f.at[pl.ds(0, n_lvl - 1)], set_recv.at[12])
+    result[1] = partial + (step1 * step0) * unpacked(r_f[...])
 
     wait(r_a.at[pl.ds(0, n_lvl - 1)], set_send.at[0])
     wait(r_coords.at[0], set_send.at[1])
@@ -522,9 +551,10 @@
     wait(r_ct.at[0], set_send.at[6])
     wait(r_ct.at[1], set_send.at[7])
     wait(r_g.at[pl.ds(0, n_lvl - 1)], set_send.at[8])
-    for kind in range(3):
-        wait(r_c.at[kind, pl.ds(0, n_leaf - 1)], set_send.at[9 + kind])
-        wait(r_d.at[kind, pl.ds(0, n_lvl - 1)], set_send.at[12 + kind])
+    wait(r_c.at[pl.ds(0, n_leaf - 1)], set_send.at[9])
+    wait(r_d.at[pl.ds(0, n_lvl - 1)], set_send.at[10])
+    wait(r_e.at[pl.ds(0, n_leaf - 1)], set_send.at[11])
+    wait(r_f.at[pl.ds(0, n_lvl - 1)], set_send.at[12])
 
     def sent(j, carry):
         wait(r1.at[j, pl.ds(0, n_lvl - 1)], send1.at[j])
@@ -569,10 +599,12 @@
     )
     scratch = [V(a.shape, a.dtype) for a in arrays] + [
         V((n_dev, 2 * pts), BF16), V((n_dev, 2 * pts), BF16),
+        V((n_lvl, n_leaf // 8 + 1, 8, LANES), F32), V((n_lvl, n_leaf // 8 + 1, 8, LANES), F32),
+        V((n_leaf, n_lvl + 1, LANES), F32), V((n_leaf, n_lvl + 1, LANES), F32),
+        V((n_leaf, 2, n_lvl, LANES), F32), V((n_leaf, 2, n_lvl, LANES), F32),
         V((n_lvl, 2, n_leaf, LANES), F32), V((n_lvl, 2, n_leaf, LANES), F32),
-        V((n_leaf, 2, n_lvl, LANES), F32), V((n_leaf, 2, n_lvl, LANES), F32),
-        V((3, n_leaf, n_lvl, LANES), F32), V((3, n_leaf, n_lvl, LANES), F32),
-        V((3, n_lvl, n_leaf, LANES), F32), V((3, n_lvl, n_leaf, LANES), F32),
+        V((n_leaf, n_lvl, LANES), F32), V((n_leaf, n_lvl, LANES), F32),
+        V((n_lvl, n_leaf, LANES), F32), V((n_lvl, n_leaf, LANES), F32),
         V((2, dim, pts), F32),
         V((2, 8, LANES), F32), V((n_lvl, 2, 8, LANES), F32),
         V((8, LANES), F32), V((n_leaf, 8, LANES), F32),
@@ -585,29 +617,31 @@
         V((pts, LANES), BF16), V((pts, LANES), BF16),
         V((LANES, pts), BF16), V((LANES, pts), BF16),
         V((2 * LANES, pts), BF16), V((2 * LANES, pts), BF16),
+        V((2 * LANES, LANES), BF16), V((2 * LANES, LANES), BF16),
         V((LANES, wide + LANES), BF16), V((LANES, wide + LANES), BF16),
-        V((APPLIES + 1, rows, pts), F32), V((rows, pts), F32),
+        V((APPLIES + 1, rows, pts), F32), V((rows, pts), F32), V((rows, LANES), F32),
         V((APPLIES, 2, rows, pts), F32), V((APPLIES - 1, rows, LANES), F32),
         V((APPLIES + 1, n_lvl, 8, LANES), F32), V((APPLIES + 1, n_lvl, 8, LANES), F32),
         V((APPLIES + 1, 8, LANES), F32), V((APPLIES + 1, n_leaf, 8, LANES), F32),
         V((APPLIES + 2, n_lvl, 2, 8, LANES), F32), V((APPLIES + 2, n_lvl, 2, 8, LANES), F32),
-        D((len(arrays),)), D((15,)), D((15,)),
+        D((len(arrays),)), D((13,)), D((13,)),
         D((APPLIES, 2)), D((APPLIES, 2)),
         D((APPLIES + 1,)), D((APPLIES + 1,)), D((APPLIES + 1,)), D((APPLIES + 1,)),
         D((APPLIES + 2,)), D((APPLIES + 2,)),
     ]
-    out = jax.ShapeDtypeStruct((rows, pts), F32)
+    out = jax.ShapeDtypeStruct((2, rows, pts), F32)
     body = lambda *refs: kernel((n_leaf, n_lvl), *refs)
-    return pl.pallas_call(
+    both = pl.pallas_call(
         body,
-        out_shape=(out, out),
+        out_shape=out,
         in_specs=[hbm] * len(arrays) + [smem] * 3,
-        out_specs=(vmem, vmem),
+        out_specs=vmem,
         scratch_shapes=scratch,
         compiler_params=pltpu.CompilerParams(
             collective_id=0, has_side_effects=True, vmem_limit_bytes=60 * 1024 * 1024
         ),
     )(*arrays, near_list, far_one, far_two)
+    return both[0], both[1]
 
 
 def solution(mesh):

time: 96.5 us -> 95.1 us (0.985)
    unnamed x4 -> x0, local copies, waits for them, and re-layouts: 2.26 us -> none
    squeeze x0 -> x1, local copies, waits for them, and re-layouts: none -> 1.69 us  [on_device(): return (both[0], both[1])]
where the time goes in v4:
time: 95.1 us; the launch traced here: 95 us
  Pallas kernels  92.7 us (97%)
  local copies, waits for them, and re-layouts  1.69 us (2%)
    pallas_call x1, Pallas kernels, on_device(): pl.pallas_call(body, out_shape=out, in_specs=[hbm] * len(arrays) + [smem]...  92.7 us

profile of v4, /device:TPU:1, one launch (start us, length us, event | category | flops | bytes accessed | tf_op | source)
XLA Modules:
  0.0 95.0 jit_solution(14730055214595347210)
XLA Ops:
  0.6 92.7 %shard_map.122 = f32[2,64,512]{2,1,0:T(8,128)} custom-call(f32[64,512]{1,0:T(8,128)} %refs_0_.1, s32[1,512]{1,0:T(1,128)} %bitcast.5, f32[8,512]{1,0:T(8,128)} %refs_2_.1, f32[4,64,128]{2,1,0:T(8,128)} %refs_3_.1, f32[4,64,64]{2,1,0:T(8,128)} %refs_4_.1, f32[1,64,64]{2,1,0:T(8,128)} %refs_5_.1, f32[1,8,64]{2,1,0:T(8,128)} %refs_6_.1, f32[1,8,64]{2,1,0:T(8,128)} %refs_7_.1, ...), custom_call_target="tpu_custom_call" | custom-call | tf_op jit(solution)/shard_map/pallas_call | solution.py:634
  93.3 1.7 %slice_bitcast_fusion = (f32[64,512]{1,0:T(8,128)}, f32[64,512]{1,0:T(8,128)}) fusion(f32[2,64,512]{2,1,0:T(8,128)} %shard_map.122), kind=kLoop, calls=%fused_computation | loop fusion | bytes 524288 | tf_op jit(solution)/shard_map/squeeze | solution.py:644

commit v5 on v4

--- a/solution.py
+++ b/solution.py
@@ -312,8 +312,8 @@
 
     def chosen(lists, get):
         lists = jnp.where(low, pltpu.roll(lists, half, 1), lists)
-        named = [jnp.broadcast_to(lists[k : k + 1], (8, LANES)) for k in range(upper_count)]
         picks = [get(0)] * upper_count
+        named = [jnp.broadcast_to(lists[k : k + 1], picks[0].shape) for k in range(upper_count)]
         for q in range(1, n_leaf):
             value = get(q)
             picks = [jnp.where(n == float(q), value, p) for n, p in zip(named, picks)]
@@ -375,17 +375,30 @@
 
     def scatter(j, value):
         s1[j] = value.reshape(n_lvl, 8, LANES)
+        over_lvl(lambda peer: s1.at[j, peer], r1.at[j, lvl], send1.at[j], recv1.at[j])
         r1[j, lvl] = s1[j, lvl]
-        over_lvl(lambda peer: s1.at[j, peer], r1.at[j, lvl], send1.at[j], recv1.at[j])
-
-    def broadcast(j, value):
+
+    def broadcast_to(j, peers):
+        for peer in peers:
+            copy(s2.at[j], r2.at[j, leaf], send2.at[j], recv2.at[j], (peer, lvl))
+
+    far_peers, near_peers = leaf_peers[:12], leaf_peers[12:]
+
+    def broadcast_far(j, lower, upper):
+        value = jnp.where(low[:4], lower[:4], upper[4:])
         s2[j] = value
+        broadcast_to(j, far_peers)
         r2[j, leaf] = value
-        over_leaf(lambda peer: s2.at[j], r2.at[j, leaf], send2.at[j], recv2.at[j])
+
+    def half_rows(a, b):
+        turned_a, turned_b = pltpu.roll(a, half, 1), pltpu.roll(b, half, 1)
+        return jnp.concatenate(
+            [jnp.where(low[:4], a, turned_b), jnp.where(low[:4], turned_a, b)], axis=0
+        )
 
     def gather(j):
+        over_lvl(lambda peer: s3.at[j, peer], r3.at[j, lvl], send3.at[j], recv3.at[j])
         r3[j, lvl] = s3[j, lvl]
-        over_lvl(lambda peer: s3.at[j, peer], r3.at[j, lvl], send3.at[j], recv3.at[j])
 
     def wait1(j):
         wait(r1.at[j, pl.ds(0, n_lvl - 1)], recv1.at[j])
@@ -429,8 +442,10 @@
     acc[...] = dot_split(wbuf[0], w_hi[pts : 2 * pts], w_lo[pts : 2 * pts])
     wait1(0)
     got = r1[0]
-    broadcast(0, jnp.sum(got, axis=0))
+    up = jnp.sum(got, axis=0)
+    broadcast_far(0, pltpu.roll(up, half, 1), up)
     send_potentials(0, level_one(got, None), zero8, (zero8, zero8))
+    broadcast_to(0, near_peers)
 
     def body(j, last):
         wait(r_halo.at[j, 0], halo_recv.at[j, 0])
@@ -455,7 +470,7 @@
         power = wbuf[j] + dot_split(jnp.where(low_rows, 0.0, main), ct_hi[...], ct_lo[...])
         square = jnp.sum(power * power, axis=1, keepdims=True)
         if last:
-            part = iota((rows, LANES), 1) // (LANES // 4)
+            part = lax.rem(iota((rows, LANES), 1), half) // (half // 4)
             sums = jnp.where(part == 3, square, 0.0)
             for k in range(3):
                 sums = jnp.where(part == k, qbuf[k + 1], sums)
@@ -477,19 +492,23 @@
         potentials = []
         for g, group in enumerate(groups):
             ups = chosen(r_top[group], lambda q: r2[j, q])
-            tiles = [jnp.where(low, pltpu.roll(ups[m], half, 1), ups[m + 1]) for m in (0, 2)]
+            tiles = [half_rows(ups[m], ups[m + 1]) for m in (0, 2)]
             potentials.append(dot_split(jnp.concatenate(tiles, axis=1), k2_hi[g], k2_lo[g]))
         f2, edges = potentials[0], potentials[1:]
         if last:
             send_potentials(j + 1, None, f2, edges)
             wait1(j + 1)
-            broadcast(j + 1, jnp.sum(r1[j + 1], axis=0))
+            sums = jnp.sum(r1[j + 1], axis=0)
+            broadcast_far(j + 1, sums, sums)
+            broadcast_to(j + 1, near_peers)
             return
         add = dot_split(f2, tg_hi[...], tg_lo[...])
         wait1(j + 1)
         got = r1[j + 1]
+        up = jnp.sum(got, axis=0) + add[:, wide:]
+        broadcast_far(j + 1, pltpu.roll(up, half, 1), up)
         send_potentials(j + 1, level_one(got, add[:, :wide]), f2, edges)
-        broadcast(j + 1, jnp.sum(got, axis=0) + add[:, wide:])
+        broadcast_to(j + 1, near_peers)
 
     def step(j, carry):
         body(j, False)
@@ -516,6 +535,7 @@
     back3 = unpacked(r_d[:, 1])
     wait2(APPLIES)
     sums = jnp.sum(r2[APPLIES], axis=0)
+    sums = jnp.concatenate([sums, pltpu.roll(sums, half, 1)], axis=0)
     for d in range(n_lvl):
         s3[APPLIES + 1, d, 0] = sums
         s3[APPLIES + 1, d, 1] = sums
@@ -527,7 +547,7 @@
 
     wait3(APPLIES + 1)
     sums = r3[APPLIES + 1, :, 0].reshape(rows, LANES)
-    g1, g2, g3, g4 = (sums[:, k * (LANES // 4) : k * (LANES // 4) + 1] for k in range(4))
+    g1, g2, g3, g4 = (sums[:, k * (half // 4) : k * (half // 4) + 1] for k in range(4))
     step0 = g1 / (g2 + RIDGE * g1 + EPSILON)
     keep = 1.0 - RIDGE * step0
     fresh = keep * keep * g1 - 2.0 * step0 * keep * g2 + step0 * step0 * g3
@@ -622,7 +642,7 @@
         V((APPLIES + 1, rows, pts), F32), V((rows, pts), F32), V((rows, LANES), F32),
         V((APPLIES, 2, rows, pts), F32), V((APPLIES - 1, rows, LANES), F32),
         V((APPLIES + 1, n_lvl, 8, LANES), F32), V((APPLIES + 1, n_lvl, 8, LANES), F32),
-        V((APPLIES + 1, 8, LANES), F32), V((APPLIES + 1, n_leaf, 8, LANES), F32),
+        V((APPLIES + 1, 4, LANES), F32), V((APPLIES + 1, n_leaf, 4, LANES), F32),
         V((APPLIES + 2, n_lvl, 2, 8, LANES), F32), V((APPLIES + 2, n_lvl, 2, 8, LANES), F32),
         D((len(arrays),)), D((13,)), D((13,)),
         D((APPLIES, 2)), D((APPLIES, 2)),

time: 95.1 us -> 91.6 us (0.963)
  Pallas kernels: 92.7 us -> 89.1 us
    pallas_call x1, Pallas kernels: 92.7 us -> 89.1 us  [on_device(): pl.pallas_call(body, out_shape=out, in_specs=[hbm] * len(arrays) + [smem]...]
where the time goes in v5:
time: 91.6 us; the launch traced here: 91.4 us
  Pallas kernels  89.1 us (97%)
  local copies, waits for them, and re-layouts  1.69 us (2%)
    pallas_call x1, Pallas kernels, on_device(): pl.pallas_call(body, out_shape=out, in_specs=[hbm] * len(arrays) + [smem]...  89.1 us

profile of v5, /device:TPU:1, one launch (start us, length us, event | category | flops | bytes accessed | tf_op | source)
XLA Modules:
  0.0 91.4 jit_solution(1123642124890338587)
XLA Ops:
  0.6 89.1 %shard_map.122 = f32[2,64,512]{2,1,0:T(8,128)} custom-call(f32[64,512]{1,0:T(8,128)} %refs_0_.1, s32[1,512]{1,0:T(1,128)} %bitcast.5, f32[8,512]{1,0:T(8,128)} %refs_2_.1, f32[4,64,128]{2,1,0:T(8,128)} %refs_3_.1, f32[4,64,64]{2,1,0:T(8,128)} %refs_4_.1, f32[1,64,64]{2,1,0:T(8,128)} %refs_5_.1, f32[1,8,64]{2,1,0:T(8,128)} %refs_6_.1, f32[1,8,64]{2,1,0:T(8,128)} %refs_7_.1, ...), custom_call_target="tpu_custom_call" | custom-call | tf_op jit(solution)/shard_map/pallas_call | solution.py:654
  89.8 1.7 %slice_bitcast_fusion = (f32[64,512]{1,0:T(8,128)}, f32[64,512]{1,0:T(8,128)}) fusion(f32[2,64,512]{2,1,0:T(8,128)} %shard_map.122), kind=kLoop, calls=%fused_computation | loop fusion | bytes 524288 | tf_op jit(solution)/shard_map/squeeze | solution.py:664

commit v6 on v5

--- a/solution.py
+++ b/solution.py
@@ -382,7 +382,7 @@
         for peer in peers:
             copy(s2.at[j], r2.at[j, leaf], send2.at[j], recv2.at[j], (peer, lvl))
 
-    far_peers, near_peers = leaf_peers[:12], leaf_peers[12:]
+    far_peers, near_peers = leaf_peers[:5], leaf_peers[5:]
 
     def broadcast_far(j, lower, upper):
         value = jnp.where(low[:4], lower[:4], upper[4:])
@@ -432,6 +432,12 @@
 
     def packed_back(value):
         return pack(oh_tree[...], value).reshape(n_leaf, n_lvl, LANES)
+
+    def return_leaf(kind, value):
+        s_c[kind] = packed_back(value)
+        r_c[kind, leaf] = s_c[kind, leaf]
+        sems = set_send.at[(9, 13)[kind]], set_recv.at[(9, 13)[kind]]
+        over_leaf(lambda p: s_c.at[kind, p], r_c.at[kind, leaf], *sems)
 
     def unpacked(rows_back):
         return unpack(oh_user[...], rows_back.reshape(n_dev, LANES))
@@ -480,13 +486,11 @@
 
             @pl.when(j == 1)
             def _():
-                s_c[:, 0] = packed_back(power)
+                return_leaf(0, power)
 
             @pl.when(j == 3)
             def _():
-                s_c[:, 1] = packed_back(power)
-                r_c[leaf] = s_c[leaf]
-                over_leaf(lambda p: s_c.at[p], r_c.at[leaf], set_send.at[9], set_recv.at[9])
+                return_leaf(1, power)
 
         wait2(j)
         potentials = []
@@ -517,9 +521,9 @@
     lax.fori_loop(0, APPLIES - 1, step, 0)
     body(APPLIES - 1, True)
 
-    wait(r_c.at[pl.ds(0, n_leaf - 1)], set_recv.at[9])
     for kind in range(2):
-        s_d[:, kind] = jnp.swapaxes(r_c[:, kind], 0, 1)
+        wait(r_c.at[kind, pl.ds(0, n_leaf - 1)], set_recv.at[(9, 13)[kind]])
+        s_d[:, kind] = jnp.swapaxes(r_c[kind], 0, 1)
     r_d[lvl] = s_d[lvl]
     over_lvl(lambda p: s_d.at[p], r_d.at[lvl], set_send.at[10], set_recv.at[10])
 
@@ -571,7 +575,8 @@
     wait(r_ct.at[0], set_send.at[6])
     wait(r_ct.at[1], set_send.at[7])
     wait(r_g.at[pl.ds(0, n_lvl - 1)], set_send.at[8])
-    wait(r_c.at[pl.ds(0, n_leaf - 1)], set_send.at[9])
+    wait(r_c.at[0, pl.ds(0, n_leaf - 1)], set_send.at[9])
+    wait(r_c.at[1, pl.ds(0, n_leaf - 1)], set_send.at[13])
     wait(r_d.at[pl.ds(0, n_lvl - 1)], set_send.at[10])
     wait(r_e.at[pl.ds(0, n_leaf - 1)], set_send.at[11])
     wait(r_f.at[pl.ds(0, n_lvl - 1)], set_send.at[12])
@@ -621,7 +626,7 @@
         V((n_dev, 2 * pts), BF16), V((n_dev, 2 * pts), BF16),
         V((n_lvl, n_leaf // 8 + 1, 8, LANES), F32), V((n_lvl, n_leaf // 8 + 1, 8, LANES), F32),
         V((n_leaf, n_lvl + 1, LANES), F32), V((n_leaf, n_lvl + 1, LANES), F32),
-        V((n_leaf, 2, n_lvl, LANES), F32), V((n_leaf, 2, n_lvl, LANES), F32),
+        V((2, n_leaf, n_lvl, LANES), F32), V((2, n_leaf, n_lvl, LANES), F32),
         V((n_lvl, 2, n_leaf, LANES), F32), V((n_lvl, 2, n_leaf, LANES), F32),
         V((n_leaf, n_lvl, LANES), F32), V((n_leaf, n_lvl, LANES), F32),
         V((n_lvl, n_leaf, LANES), F32), V((n_lvl, n_leaf, LANES), F32),
@@ -644,7 +649,7 @@
         V((APPLIES + 1, n_lvl, 8, LANES), F32), V((APPLIES + 1, n_lvl, 8, LANES), F32),
         V((APPLIES + 1, 4, LANES), F32), V((APPLIES + 1, n_leaf, 4, LANES), F32),
         V((APPLIES + 2, n_lvl, 2, 8, LANES), F32), V((APPLIES + 2, n_lvl, 2, 8, LANES), F32),
-        D((len(arrays),)), D((13,)), D((13,)),
+        D((len(arrays),)), D((14,)), D((14,)),
         D((APPLIES, 2)), D((APPLIES, 2)),
         D((APPLIES + 1,)), D((APPLIES + 1,)), D((APPLIES + 1,)), D((APPLIES + 1,)),
         D((APPLIES + 2,)), D((APPLIES + 2,)),

time: 91.6 us -> 90 us (0.983)
  Pallas kernels: 89.1 us -> 87.6 us
    pallas_call x1, Pallas kernels: 89.1 us -> 87.6 us  [on_device(): pl.pallas_call(body, out_shape=out, in_specs=[hbm] * len(arrays) + [smem]...]
where the time goes in v6:
time: 90 us; the launch traced here: 89.9 us
  Pallas kernels  87.6 us (97%)
  local copies, waits for them, and re-layouts  1.69 us (2%)
    pallas_call x1, Pallas kernels, on_device(): pl.pallas_call(body, out_shape=out, in_specs=[hbm] * len(arrays) + [smem]...  87.6 us

profile of v6, /device:TPU:1, one launch (start us, length us, event | category | flops | bytes accessed | tf_op | source)
XLA Modules:
  0.0 89.9 jit_solution(3756405096348910074)
XLA Ops:
  0.6 87.6 %shard_map.122 = f32[2,64,512]{2,1,0:T(8,128)} custom-call(f32[64,512]{1,0:T(8,128)} %refs_0_.1, s32[1,512]{1,0:T(1,128)} %bitcast.5, f32[8,512]{1,0:T(8,128)} %refs_2_.1, f32[4,64,128]{2,1,0:T(8,128)} %refs_3_.1, f32[4,64,64]{2,1,0:T(8,128)} %refs_4_.1, f32[1,64,64]{2,1,0:T(8,128)} %refs_5_.1, f32[1,8,64]{2,1,0:T(8,128)} %refs_6_.1, f32[1,8,64]{2,1,0:T(8,128)} %refs_7_.1, ...), custom_call_target="tpu_custom_call" | custom-call | tf_op jit(solution)/shard_map/pallas_call | solution.py:659
  88.2 1.7 %slice_bitcast_fusion = (f32[64,512]{1,0:T(8,128)}, f32[64,512]{1,0:T(8,128)}) fusion(f32[2,64,512]{2,1,0:T(8,128)} %shard_map.122), kind=kLoop, calls=%fused_computation | loop fusion | bytes 524288 | tf_op jit(solution)/shard_map/squeeze | solution.py:669

commit v7 on v6

--- a/solution.py
+++ b/solution.py
@@ -521,12 +521,6 @@
     lax.fori_loop(0, APPLIES - 1, step, 0)
     body(APPLIES - 1, True)
 
-    for kind in range(2):
-        wait(r_c.at[kind, pl.ds(0, n_leaf - 1)], set_recv.at[(9, 13)[kind]])
-        s_d[:, kind] = jnp.swapaxes(r_c[kind], 0, 1)
-    r_d[lvl] = s_d[lvl]
-    over_lvl(lambda p: s_d.at[p], r_d.at[lvl], set_send.at[10], set_recv.at[10])
-
     wait3(APPLIES)
     main = r3[APPLIES, :, 0].reshape(rows, LANES)
     s_e[...] = packed_back(
@@ -534,9 +528,11 @@
     )
     r_e[leaf] = s_e[leaf]
     over_leaf(lambda p: s_e.at[p], r_e.at[leaf], set_send.at[11], set_recv.at[11])
-    wait(r_d.at[pl.ds(0, n_lvl - 1)], set_recv.at[10])
-    back1 = unpacked(r_d[:, 0])
-    back3 = unpacked(r_d[:, 1])
+    for kind in range(2):
+        wait(r_c.at[kind, pl.ds(0, n_leaf - 1)], set_recv.at[(9, 13)[kind]])
+        s_d[:, kind] = jnp.swapaxes(r_c[kind], 0, 1)
+    r_d[lvl] = s_d[lvl]
+    over_lvl(lambda p: s_d.at[p], r_d.at[lvl], set_send.at[10], set_recv.at[10])
     wait2(APPLIES)
     sums = jnp.sum(r2[APPLIES], axis=0)
     sums = jnp.concatenate([sums, pltpu.roll(sums, half, 1)], axis=0)
@@ -549,6 +545,9 @@
     r_f[lvl] = s_f[lvl]
     over_lvl(lambda p: s_f.at[p], r_f.at[lvl], set_send.at[12], set_recv.at[12])
 
+    wait(r_d.at[pl.ds(0, n_lvl - 1)], set_recv.at[10])
+    back1 = unpacked(r_d[:, 0])
+    back3 = unpacked(r_d[:, 1])
     wait3(APPLIES + 1)
     sums = r3[APPLIES + 1, :, 0].reshape(rows, LANES)
     g1, g2, g3, g4 = (sums[:, k * (half // 4) : k * (half // 4) + 1] for k in range(4))

time: 90 us -> 89.4 us (level)
  no operation moved by 1% of the time
where the time goes in v7:
time: 89.4 us; the launch traced here: 89.2 us
  Pallas kernels  86.9 us (97%)
  local copies, waits for them, and re-layouts  1.69 us (2%)
    pallas_call x1, Pallas kernels, on_device(): pl.pallas_call(body, out_shape=out, in_specs=[hbm] * len(arrays) + [smem]...  86.9 us

profile of v7, /device:TPU:1, one launch (start us, length us, event | category | flops | bytes accessed | tf_op | source)
XLA Modules:
  0.0 89.2 jit_solution(11690853350291781201)
XLA Ops:
  0.6 86.9 %shard_map.122 = f32[2,64,512]{2,1,0:T(8,128)} custom-call(f32[64,512]{1,0:T(8,128)} %refs_0_.1, s32[1,512]{1,0:T(1,128)} %bitcast.5, f32[8,512]{1,0:T(8,128)} %refs_2_.1, f32[4,64,128]{2,1,0:T(8,128)} %refs_3_.1, f32[4,64,64]{2,1,0:T(8,128)} %refs_4_.1, f32[1,64,64]{2,1,0:T(8,128)} %refs_5_.1, f32[1,8,64]{2,1,0:T(8,128)} %refs_6_.1, f32[1,8,64]{2,1,0:T(8,128)} %refs_7_.1, ...), custom_call_target="tpu_custom_call" | custom-call | tf_op jit(solution)/shard_map/pallas_call | solution.py:658
  87.5 1.7 %slice_bitcast_fusion = (f32[64,512]{1,0:T(8,128)}, f32[64,512]{1,0:T(8,128)}) fusion(f32[2,64,512]{2,1,0:T(8,128)} %shard_map.122), kind=kLoop, calls=%fused_computation | loop fusion | bytes 524288 | tf_op jit(solution)/shard_map/squeeze | solution.py:668
